TPU v7x, 32 devices: a whole 2x2x4 slice. The times are simulated.
32 devices in a mesh: stream: 4 (over y, x), blk: 8 (over z, core).
Axes of the slice: x: 2, y: 2, z: 4, core: 2. Of those that a mesh axis runs over, the one named last changes fastest.
Arguments:
- latents: bfloat16 [16384, 1152], P(('stream', 'blk')), may hold values from -6 to 6
- skip_input: bfloat16 [16384, 1152], P(('stream', 'blk')), may hold values from -6 to 6
- cond_tokens: bfloat16 [64, 2, 1152], P('stream'), may hold values from -6 to 6
- extra_length: int32 [4, 16], P('stream'), may hold values from 1 to 129, 1040 in all within a row
- skip_weight: bfloat16 [2304, 1152], P('blk'), may hold values from -0.125 to 0.125
- skip_bias: bfloat16 [1152], P('blk'), may hold values from -1.75 to 1.75
- first_gain: bfloat16 [1152], P('blk'), may hold values from 0.25 to 1.75
- first_shift: bfloat16 [1152], P('blk'), may hold values from -1.75 to 1.75
- joint_weight: bfloat16 [1152, 3456], P('blk'), may hold values from -0.1875 to 0.1875
- out_weight: bfloat16 [1152, 1152], P('blk'), may hold values from -1.5 to 1.5
- out_bias: bfloat16 [1152], P('blk'), may hold values from -1.75 to 1.75
- second_gain: bfloat16 [1152], P('blk'), may hold values from 0.25 to 1.75
- second_shift: bfloat16 [1152], P('blk'), may hold values from -1.75 to 1.75
- up_weight: bfloat16 [1152, 4608], P('blk'), may hold values from -0.1875 to 0.1875
- up_bias: bfloat16 [4608], P('blk'), may hold values from -1.75 to 1.75
- down_weight: bfloat16 [4608, 1152], P('blk'), may hold values from -0.09375 to 0.09375
- down_bias: bfloat16 [1152], P('blk'), may hold values from -1.75 to 1.75
- cotangent: bfloat16 [16384, 1152], P(('stream', 'blk')), may hold values from -6 to 6
Outputs:
- output_tokens: bfloat16 [16384, 1152], P(('stream', 'blk'))
- latents_grad: bfloat16 [16384, 1152], P(('stream', 'blk'))
- skip_grad: bfloat16 [16384, 1152], P(('stream', 'blk'))
- cond_grad: bfloat16 [64, 2, 1152], P('stream')
- grad_skip_weight: float32 [2304, 1152], P('blk')
- grad_skip_bias: float32 [1152], P('blk')
- grad_first_gain: float32 [1152], P('blk')
- grad_first_shift: float32 [1152], P('blk')
- grad_joint_weight: float32 [1152, 3456], P('blk')
- grad_out_weight: float32 [1152, 1152], P('blk')
- grad_out_bias: float32 [1152], P('blk')
- grad_second_gain: float32 [1152], P('blk')
- grad_second_shift: float32 [1152], P('blk')
- grad_up_weight: float32 [1152, 4608], P('blk')
- grad_up_bias: float32 [4608], P('blk')
- grad_down_weight: float32 [4608, 1152], P('blk')
- grad_down_bias: float32 [1152], P('blk')
Inputs may be any that keep to these rules, and one draw needn't show every extreme that they name: In each stream the item lengths extra_length + 191 sum to 4096, and one item has exactly 320 tokens.
All inputs are finite; a program needn't handle non-finite values.
Results may differ from a plain program's by a relative error of at most 0.02.
Values may be sent and summed in bfloat16 or wider, within the bound.
A program may use at most 256 MiB of HBM per device.

v0:
```python
from functools import partial

import jax
import jax.numpy as jnp
from jax import lax
from jax.sharding import PartitionSpec as P

HEADS = 16
HEAD = 72
LEN_MIN = 192


def shifted(value, axis, steps):
    count = lax.axis_size(axis)
    leading, last = (max(0, -steps), min(count, count - steps))
    return lax.ppermute(value, axis, [(source, source + steps) for source in range(leading, last)])


def layer_norm(values, gain, shift):
    center = values - jnp.mean(values, axis=-1, keepdims=True)
    spread = jnp.mean(center * center, axis=-1, keepdims=True)
    return center * lax.rsqrt(spread + 1e-05) * gain + shift


def contract_rows(left, right):
    return lax.dot_general(
        left, right, (((0,), (0,)), ((), ())), preferred_element_type=jnp.float32
    )


def contract_cols(left, right):
    return lax.dot_general(
        left, right, (((1,), (1,)), ((), ())), preferred_element_type=jnp.float32
    )


def segment_ids(ends, places):
    inside = jnp.sum((ends[None, :] <= places[:, None]).astype(jnp.int32), axis=1)
    return jnp.where(places >= 0, inside, -1)


def split_heads(block):
    return block.reshape(block.shape[0], HEADS, HEAD).transpose(1, 0, 2)


def merge_heads(block):
    return block.transpose(1, 0, 2).reshape(block.shape[1], HEADS * HEAD)


def masked_scores(query, keys, allowed):
    scores = contract_cols(query, keys) * HEAD ** (-0.5)
    return jnp.where(allowed, scores, -1e30)


def shards(
    latents,
    skip_input,
    cond_tokens,
    extra_length,
    skip_weight,
    skip_bias,
    first_gain,
    first_shift,
    joint_weight,
    out_weight,
    out_bias,
    second_gain,
    second_shift,
    up_weight,
    up_bias,
    down_weight,
    down_bias,
    cotangent,
):
    whole = (
        lax.all_gather(skip_weight, "blk", axis=0, tiled=True),
        lax.all_gather(skip_bias, "blk", axis=0, tiled=True),
        lax.all_gather(first_gain, "blk", axis=0, tiled=True),
        lax.all_gather(first_shift, "blk", axis=0, tiled=True),
        lax.all_gather(joint_weight, "blk", axis=0, tiled=True),
        lax.all_gather(out_weight, "blk", axis=0, tiled=True),
        lax.all_gather(out_bias, "blk", axis=0, tiled=True),
        lax.all_gather(second_gain, "blk", axis=0, tiled=True),
        lax.all_gather(second_shift, "blk", axis=0, tiled=True),
        lax.all_gather(up_weight, "blk", axis=0, tiled=True),
        lax.all_gather(up_bias, "blk", axis=0, tiled=True),
        lax.all_gather(down_weight, "blk", axis=0, tiled=True),
        lax.all_gather(down_bias, "blk", axis=0, tiled=True),
    )
    (
        skip_matrix,
        skip_offset,
        gain_first,
        shift_first,
        joint_matrix,
        out_matrix,
        out_offset,
        gain_second,
        shift_second,
        up_matrix,
        up_offset,
        down_matrix,
        down_offset,
    ) = whole
    rows = latents.shape[0]
    width = latents.shape[1]
    scale = HEAD ** (-0.5)
    joined = jnp.concatenate([latents, skip_input], 1)
    base = jnp.dot(joined, skip_matrix, preferred_element_type=jnp.float32) + skip_offset
    first_in = layer_norm(base, gain_first, shift_first).astype(jnp.bfloat16)
    triple = jnp.dot(first_in, joint_matrix, preferred_element_type=jnp.float32).astype(
        jnp.bfloat16
    )
    query = triple[:, :width]
    pair_here = triple[:, width:]
    pair_left = shifted(pair_here, "blk", 1)
    cond_flat = cond_tokens.reshape(-1, width).astype(jnp.float32)
    cond_in = layer_norm(cond_flat, gain_first, shift_first).astype(jnp.bfloat16)
    cond_pair = jnp.dot(
        cond_in, joint_matrix[:, width:], preferred_element_type=jnp.float32
    ).astype(jnp.bfloat16)
    pairs = jnp.concatenate([pair_left, pair_here, cond_pair], 0)
    ends = jnp.cumsum(extra_length[0] + (LEN_MIN - 1))
    here = lax.axis_index("blk")
    places = here * rows + lax.iota(jnp.int32, rows)
    seg_here = segment_ids(ends, places)
    seg_left = segment_ids(ends, places - rows)
    cond_seg = lax.iota(jnp.int32, cond_pair.shape[0]) // 2
    allowed = seg_here[:, None] == jnp.concatenate([seg_left, seg_here, cond_seg])[None, :]
    head_query = split_heads(query)
    head_key = split_heads(pairs[:, :width])
    head_value = split_heads(pairs[:, width:])

    def head_forward(parts):
        query_one, key_one, value_one = parts
        scores = masked_scores(query_one, key_one, allowed)
        top = jnp.max(scores, axis=1, keepdims=True)
        expo = jnp.exp(scores - top)
        total = jnp.sum(expo, axis=1, keepdims=True)
        probs = (expo / total).astype(jnp.bfloat16)
        mixed = jnp.dot(probs, value_one, preferred_element_type=jnp.float32)
        return (mixed, (top + jnp.log(total))[:, 0])

    mixed, logsum = lax.map(head_forward, (head_query, head_key, head_value))
    attended = merge_heads(mixed).astype(jnp.bfloat16)
    middle = base + jnp.dot(attended, out_matrix, preferred_element_type=jnp.float32) + out_offset
    second_in = layer_norm(middle, gain_second, shift_second).astype(jnp.bfloat16)
    before = jnp.dot(second_in, up_matrix, preferred_element_type=jnp.float32) + up_offset
    hidden = jax.nn.gelu(before, approximate=False).astype(jnp.bfloat16)
    output = middle + jnp.dot(hidden, down_matrix, preferred_element_type=jnp.float32) + down_offset
    again = (
        lax.all_gather(skip_weight, "blk", axis=0, tiled=True),
        lax.all_gather(skip_bias, "blk", axis=0, tiled=True),
        lax.all_gather(first_gain, "blk", axis=0, tiled=True),
        lax.all_gather(first_shift, "blk", axis=0, tiled=True),
        lax.all_gather(joint_weight, "blk", axis=0, tiled=True),
        lax.all_gather(out_weight, "blk", axis=0, tiled=True),
        lax.all_gather(out_bias, "blk", axis=0, tiled=True),
        lax.all_gather(second_gain, "blk", axis=0, tiled=True),
        lax.all_gather(second_shift, "blk", axis=0, tiled=True),
        lax.all_gather(up_weight, "blk", axis=0, tiled=True),
        lax.all_gather(up_bias, "blk", axis=0, tiled=True),
        lax.all_gather(down_weight, "blk", axis=0, tiled=True),
        lax.all_gather(down_bias, "blk", axis=0, tiled=True),
    )
    (
        skip_matrix,
        skip_offset,
        gain_first,
        shift_first,
        joint_matrix,
        out_matrix,
        out_offset,
        gain_second,
        shift_second,
        up_matrix,
        up_offset,
        down_matrix,
        down_offset,
    ) = again
    incoming = cotangent.astype(jnp.float32)
    grad_down_offset = jnp.sum(incoming, axis=0)
    grad_down_matrix = contract_rows(hidden, cotangent)
    d_hidden = contract_cols(cotangent, down_matrix)
    gelu_value, gelu_pull = jax.vjp(partial(jax.nn.gelu, approximate=False), before)
    d_before = gelu_pull(d_hidden)[0].astype(jnp.bfloat16)
    grad_up_offset = jnp.sum(d_before.astype(jnp.float32), axis=0)
    grad_up_matrix = contract_rows(second_in, d_before)
    d_second = contract_cols(d_before, up_matrix)
    norm_value, norm_pull = jax.vjp(
        layer_norm, middle, gain_second.astype(jnp.float32), shift_second.astype(jnp.float32)
    )
    d_middle_norm, grad_gain_second, grad_shift_second = norm_pull(d_second)
    d_middle = incoming + d_middle_norm
    d_branch = d_middle.astype(jnp.bfloat16)
    grad_out_offset = jnp.sum(d_branch.astype(jnp.float32), axis=0)
    grad_out_matrix = contract_rows(attended, d_branch)
    d_attended = contract_cols(d_branch, out_matrix).astype(jnp.bfloat16)

    def head_backward(parts):
        query_one, key_one, value_one, grad_one, logsum_one = parts
        scores = masked_scores(query_one, key_one, allowed)
        probs = jnp.exp(scores - logsum_one[:, None])
        d_probs = contract_cols(grad_one, value_one)
        inner = jnp.sum(probs * d_probs, axis=1, keepdims=True)
        d_scores = (probs * (d_probs - inner)).astype(jnp.bfloat16)
        d_query_one = jnp.dot(d_scores, key_one, preferred_element_type=jnp.float32) * scale
        d_key_one = contract_rows(d_scores, query_one) * scale
        d_value_one = contract_rows(probs.astype(jnp.bfloat16), grad_one)
        return (d_query_one, d_key_one, d_value_one)

    d_query_heads, d_key_heads, d_value_heads = lax.map(
        head_backward, (head_query, head_key, head_value, split_heads(d_attended), logsum)
    )
    d_query = merge_heads(d_query_heads)
    d_pairs = jnp.concatenate([merge_heads(d_key_heads), merge_heads(d_value_heads)], 1)
    d_left = d_pairs[:rows]
    d_own = d_pairs[rows : 2 * rows]
    d_cond_part = d_pairs[2 * rows :]
    d_returned = shifted(d_left.astype(jnp.bfloat16), "blk", -1).astype(d_left.dtype)
    d_cond_total = lax.psum(d_cond_part.astype(jnp.bfloat16), "blk")
    d_triple = jnp.concatenate([d_query, d_own + d_returned], 1).astype(jnp.bfloat16)
    leading = (here == 0).astype(jnp.float32)
    cond_term = contract_rows(cond_in, d_cond_total) * leading
    grad_joint_matrix = contract_rows(first_in, d_triple) + jnp.concatenate(
        [jnp.zeros((width, width), jnp.float32), cond_term], 1
    )
    d_first = contract_cols(d_triple, joint_matrix)
    d_cond_in = contract_cols(d_cond_total, joint_matrix[:, width:])
    first_value, first_pull = jax.vjp(
        layer_norm, base, gain_first.astype(jnp.float32), shift_first.astype(jnp.float32)
    )
    d_base_norm, grad_gain_tokens, grad_shift_tokens = first_pull(d_first)
    cond_value, cond_pull = jax.vjp(
        layer_norm, cond_flat, gain_first.astype(jnp.float32), shift_first.astype(jnp.float32)
    )
    d_cond_flat, grad_gain_cond, grad_shift_cond = cond_pull(d_cond_in)
    grad_gain_first = grad_gain_tokens + leading * grad_gain_cond
    grad_shift_first = grad_shift_tokens + leading * grad_shift_cond
    d_base = (d_middle + d_base_norm).astype(jnp.bfloat16)
    grad_skip_offset = jnp.sum(d_base.astype(jnp.float32), axis=0)
    grad_skip_matrix = contract_rows(joined, d_base)
    d_joined = contract_cols(d_base, skip_matrix)
    shares = (
        lax.psum_scatter(
            grad_skip_matrix.astype(jnp.bfloat16), "blk", scatter_dimension=0, tiled=True
        ).astype(jnp.float32),
        lax.psum_scatter(
            grad_skip_offset.astype(jnp.bfloat16), "blk", scatter_dimension=0, tiled=True
        ).astype(jnp.float32),
        lax.psum_scatter(
            grad_gain_first.astype(jnp.bfloat16), "blk", scatter_dimension=0, tiled=True
        ).astype(jnp.float32),
        lax.psum_scatter(
            grad_shift_first.astype(jnp.bfloat16), "blk", scatter_dimension=0, tiled=True
        ).astype(jnp.float32),
        lax.psum_scatter(
            grad_joint_matrix.astype(jnp.bfloat16), "blk", scatter_dimension=0, tiled=True
        ).astype(jnp.float32),
        lax.psum_scatter(
            grad_out_matrix.astype(jnp.bfloat16), "blk", scatter_dimension=0, tiled=True
        ).astype(jnp.float32),
        lax.psum_scatter(
            grad_out_offset.astype(jnp.bfloat16), "blk", scatter_dimension=0, tiled=True
        ).astype(jnp.float32),
        lax.psum_scatter(
            grad_gain_second.astype(jnp.bfloat16), "blk", scatter_dimension=0, tiled=True
        ).astype(jnp.float32),
        lax.psum_scatter(
            grad_shift_second.astype(jnp.bfloat16), "blk", scatter_dimension=0, tiled=True
        ).astype(jnp.float32),
        lax.psum_scatter(
            grad_up_matrix.astype(jnp.bfloat16), "blk", scatter_dimension=0, tiled=True
        ).astype(jnp.float32),
        lax.psum_scatter(
            grad_up_offset.astype(jnp.bfloat16), "blk", scatter_dimension=0, tiled=True
        ).astype(jnp.float32),
        lax.psum_scatter(
            grad_down_matrix.astype(jnp.bfloat16), "blk", scatter_dimension=0, tiled=True
        ).astype(jnp.float32),
        lax.psum_scatter(
            grad_down_offset.astype(jnp.bfloat16), "blk", scatter_dimension=0, tiled=True
        ).astype(jnp.float32),
    )
    (
        share_skip,
        share_skip_offset,
        share_gain_first,
        share_shift_first,
        share_joint,
        share_out,
        share_out_offset,
        share_gain_second,
        share_shift_second,
        share_up,
        share_up_offset,
        share_down,
        share_down_offset,
    ) = shares
    summed = (
        lax.psum(share_skip.astype(jnp.bfloat16), "stream").astype(jnp.float32),
        lax.psum(share_skip_offset.astype(jnp.bfloat16), "stream").astype(jnp.float32),
        lax.psum(share_gain_first.astype(jnp.bfloat16), "stream").astype(jnp.float32),
        lax.psum(share_shift_first.astype(jnp.bfloat16), "stream").astype(jnp.float32),
        lax.psum(share_joint.astype(jnp.bfloat16), "stream").astype(jnp.float32),
        lax.psum(share_out.astype(jnp.bfloat16), "stream").astype(jnp.float32),
        lax.psum(share_out_offset.astype(jnp.bfloat16), "stream").astype(jnp.float32),
        lax.psum(share_gain_second.astype(jnp.bfloat16), "stream").astype(jnp.float32),
        lax.psum(share_shift_second.astype(jnp.bfloat16), "stream").astype(jnp.float32),
        lax.psum(share_up.astype(jnp.bfloat16), "stream").astype(jnp.float32),
        lax.psum(share_up_offset.astype(jnp.bfloat16), "stream").astype(jnp.float32),
        lax.psum(share_down.astype(jnp.bfloat16), "stream").astype(jnp.float32),
        lax.psum(share_down_offset.astype(jnp.bfloat16), "stream").astype(jnp.float32),
    )
    return (
        output.astype(jnp.bfloat16),
        d_joined[:, :width].astype(jnp.bfloat16),
        d_joined[:, width:].astype(jnp.bfloat16),
        d_cond_flat.reshape(cond_tokens.shape).astype(jnp.bfloat16),
        summed[0],
        summed[1],
        summed[2],
        summed[3],
        summed[4],
        summed[5],
        summed[6],
        summed[7],
        summed[8],
        summed[9],
        summed[10],
        summed[11],
        summed[12],
    )


def solution(mesh):
    placed = (
        P(("stream", "blk"), None),
        P(("stream", "blk"), None),
        P("stream", None, None),
        P("stream", None),
        P("blk", None),
        P("blk"),
        P("blk"),
        P("blk"),
        P("blk", None),
        P("blk", None),
        P("blk"),
        P("blk"),
        P("blk"),
        P("blk", None),
        P("blk"),
        P("blk", None),
        P("blk"),
        P(("stream", "blk"), None),
    )
    return jax.shard_map(
        shards,
        mesh=mesh,
        in_specs=placed,
        out_specs=(
            P(("stream", "blk"), None),
            P(("stream", "blk"), None),
            P(("stream", "blk"), None),
            P("stream", None, None),
            P("blk", None),
            P("blk"),
            P("blk"),
            P("blk"),
            P("blk", None),
            P("blk", None),
            P("blk"),
            P("blk"),
            P("blk"),
            P("blk", None),
            P("blk"),
            P("blk", None),
            P("blk"),
        ),
        check_vma=False,
    )
```

profile of v0, /device:TPU:12, one launch (start us, length us, event | category | flops | bytes accessed | tf_op | source)
XLA Modules:
  0.0 1217.4 jit_solution(15284143598580252437)
XLA Ops:
  13.8 26.6 %all-reduce.18 = (bf16[1152]{0:T(1024)(128)(2,1)S(1)}, bf16[1152]{0:T(1024)(128)(2,1)S(1)}, bf16[1152]{0:T(1024)(128)(2,1)S(1)}, bf16[1152]{0:T(1024)(128)(2,1)S...) all-reduce(bf16[1152]{0:T(1024)(128)(2,1)S(1)} %dynamic-update-slic, ...), channel_id=1, replica_groups=mesh['stream'=4,'blk'=8] {'blk'}, use_global_device_ids=true, to_apply=%add.1 | all-reduce | flops 11520 | bytes 46080
  42.7 23.8 %all-gather.6.cloned.1.call-done = bf16[2304,1152]{1,0:T(8,128)(2,1)} async-done(((bf16[288,1152]{1,0:T(8,128)(2,1)}), bf16[2304,1152]{1,0:T(8,128)(2,1)}) %all-gather.6.cloned.1.call-update) | async-done | bytes 5308432 | tf_op jit(solution)/shard_map/all_gather | solution.py:76
  66.5 6.5 fusion.86
  73.5 71.5 %all-gather.8.cloned.1.call-done = bf16[1152,3456]{1,0:T(8,128)(2,1)} async-done(((bf16[144,3456]{1,0:T(8,128)(2,1)}), bf16[1152,3456]{1,0:T(8,128)(2,1)}) %all-gather.8.cloned.1.call-update) | async-done | bytes 7962640 | tf_op jit(solution)/shard_map/all_gather | solution.py:80
  145.0 8.7 convolution_convert_fusion.4
  168.9 44.1 %collective-permute-done = bf16[512,2304]{1,0:T(8,128)(2,1)} collective-permute-done((bf16[512,2304]{1,0:T(8,128)(2,1)}, bf16[512,2304]{1,0:T(8,128)(2,1)}, u32[]{:S(2)}, u32[]{:S(2)}) %collective-permute-start) | collective-permute-done | bytes 2359328 | tf_op jit(solution)/shard_map/ppermute | solution.py:16
  235.0 74.7 %while.28 = (s32[]{:T(128)}, bf16[16,512,72]{1,2,0:T(8,128)(2,1)S(1)}, f32[16,512]{1,0:T(8,128)}, bf16[16,512,72]{2,1,0:T(8,128)(2,1)}, bf16[16,1056,72]{2,1,0:T...) while((s32[]{:T(128)}, ...), condition=%wide.region_10.11_spmd.clone, body=%wide.region_7.10_spmd.clone.sunk | while | flops 160579072 | bytes 7336177 | solution.py:144
  309.7 5.0 fusion.87
  316.4 13.3 %fusion.73 = f32[512,4608]{1,0:T(8,128)} fusion(bf16[1152,4608]{1,0:T(8,128)(2,1)} %all-gather.12.cloned.1.call-done, f32[512,1152]{1,0:T(8,128)S(1)} %get-tuple-element.322, f32[1152]{0:T(1024)} %convert_element_type.232, f32[1152]{0:T(1024)S(1)} %copy-done.30, f32[512]{0:T(512)} %fusion.70, f32[512]{0:T(512)} %copy-done.34), kind=kOutput, calls=%fused_computation.155 | convolution fusion | flops 5438767104 | bytes 22426624 | tf_op jit(solution)/shard_map/dot_general | solution.py:148
  329.7 61.5 %all-gather.14.cloned.1.call-done = bf16[4608,1152]{1,0:T(8,128)(2,1)} async-done(((bf16[576,1152]{1,0:T(8,128)(2,1)}), bf16[4608,1152]{1,0:T(8,128)(2,1)}) %all-gather.14.cloned.1.call-update) | async-done | bytes 10616848 | tf_op jit(solution)/shard_map/all_gather | solution.py:87
  391.2 31.9 %fusion.75 = (bf16[4608]{0:T(1024)(128)(2,1)}, bf16[512,4608]{1,0:T(8,128)(2,1)S(1)}, f32[512,4608]{1,0:T(8,128)}) fusion(f32[512,4608]{1,0:T(8,128)} %fusion.73, f32[4608]{0:T(1024)} %convert_element_type.234, bf16[512,1152]{1,0:T(8,128)(2,1)S(1)} %copy-done.7, bf16[4608,1152]{1,0:T(8,128)(2,1)} %all-gather.14.cloned.1.call-done), kind=kOutput, calls=%fused_computation.157 | convolution fusion | flops 5610401280 | bytes 35417088 | tf_op jit(solution)/shard_map/dot_general | solution.py:32
  423.0 12.9 %multiply_reduce_fusion.1 = (bf16[1152]{0:T(1024)(128)(2,1)}, f32[512]{0:T(512)S(1)}, bf16[1152]{0:T(1024)(128)(2,1)}, f32[512,1152]{1,0:T(8,128)S(1)}) fusion(f32[512,1152]{1,0:T(8,128)S(1)} %get-tuple-element.322, f32[512]{0:T(512)S(1)} %copy-done.48, f32[512]{0:T(512)S(1)} %copy-done.35, f32[1152]{0:T(1024)S(1)} %copy-done.30, ...), kind=kOutput, calls=%fused_computation.104 | convolution fusion | flops 5440534016 | bytes 20069376 | tf_op jit(solution)/shard_map/dot_general | solution.py:32
  445.3 156.3 %while.29 = (s32[]{:T(128)}, bf16[16,512,72]{1,2,0:T(8,128)(2,1)}, f32[16,1056,72]{1,2,0:T(8,128)}, f32[16,1056,72]{1,2,0:T(8,128)}, bf16[16,512,72]{2,1,0:T(8,1...) while((s32[]{:T(128)}, bf16[16,512,72]{1,2,0:T(8,128)(2,1)}, ...), condition=%wide.region_17.18_spmd.clone, body=%wide.region_15.17_spmd.clone.sunk | while | flops 394802944 | bytes 18273536 | solution.py:212
  601.6 7.0 fusion.46
  611.9 4.9 collective-permute-start.1
  623.4 25.6 %collective-permute-done.1 = bf16[512,2304]{0,1:T(8,128)(2,1)} collective-permute-done((bf16[512,2304]{0,1:T(8,128)(2,1)}, bf16[512,2304]{0,1:T(8,128)(2,1)}, u32[]{:S(2)}, u32[]{:S(2)}) %collective-permute-start.1) | collective-permute-done | bytes 2359328 | tf_op jit(solution)/shard_map/ppermute | solution.py:16
  653.0 10.3 multiply_reduce_fusion.2
  667.7 7.2 convolution_convert_fusion.2
  675.7 6.7 convolution_multiply_fusion.4
  682.4 14.1 %fusion.45 = bf16[1152,3456]{1,0:T(8,128)(2,1)} fusion(f32[1152,2304]{1,0:T(8,128)} %convolution_multiply_fusion.4, bf16[512,2304]{0,1:T(8,128)(2,1)} %copy-done.10, bf16[512,1152]{0,1:T(8,128)(2,1)} %bitcast.158, f32[512,1152]{1,0:T(8,128)} %copy-done, f32[1152]{0:T(1024)S(1)} %copy-done.29, f32[1152]{0:T(1024)S(1)} %copy-done.25, f32[512]{0:T(512)} %copy-done.46, ...), kind=kOutput, calls=%fused_computation.58 | convolution fusion | flops 4094853120 | bytes 24491008 | tf_op jit(solution)/shard_map/dot_general | solution.py:26
  697.2 10.7 convolution_convert_fusion.1
  708.4 10.8 multiply_convert_fusion.1
  719.2 12.1 convolution_convert_fusion
  733.1 41.1 %reduce-scatter.6.cloned.1.call-done = bf16[288,1152]{1,0:T(8,128)(2,1)} async-done(((bf16[2304,1152]{1,0:T(8,128)(2,1)}), bf16[288,1152]{1,0:T(8,128)(2,1)}) %reduce-scatter.6.cloned.1.call-update) | async-done | bytes 663568 | tf_op jit(solution)/shard_map/reduce_scatter | solution.py:245
  774.3 86.6 %reduce-scatter.8.cloned.1.call-done = bf16[144,3456]{1,0:T(8,128)(2,1)} async-done(((bf16[1152,3456]{1,0:T(8,128)(2,1)}), bf16[144,3456]{1,0:T(8,128)(2,1)}) %reduce-scatter.8.cloned.1.call-update) | async-done | bytes 995344 | tf_op jit(solution)/shard_map/reduce_scatter | solution.py:257
  860.8 111.3 %reduce-scatter.12.cloned.1.call-done = bf16[144,4608]{1,0:T(8,128)(2,1)} async-done(((bf16[1152,4608]{1,0:T(8,128)(2,1)}), bf16[144,4608]{1,0:T(8,128)(2,1)}) %reduce-scatter.12.cloned.1.call-update) | async-done | bytes 1327120 | tf_op jit(solution)/shard_map/reduce_scatter | solution.py:272
  972.1 111.4 %reduce-scatter.14.cloned.1.call-done = bf16[576,1152]{1,0:T(8,128)(2,1)} async-done(((bf16[4608,1152]{1,0:T(8,128)(2,1)}), bf16[576,1152]{1,0:T(8,128)(2,1)}) %reduce-scatter.14.cloned.1.call-update) | async-done | bytes 1327120 | tf_op jit(solution)/shard_map/reduce_scatter | solution.py:278
  1089.0 25.7 %all-reduce.17 = (bf16[1152]{0:T(1024)(128)(2,1)S(1)}, bf16[1152]{0:T(1024)(128)(2,1)S(1)}, bf16[1152]{0:T(1024)(128)(2,1)S(1)}, bf16[1152]{0:T(1024)(128)(2,1)S...) all-reduce(bf16[1152]{0:T(1024)(128)(2,1)S(1)} %dynamic-update-slic, ...), channel_id=1, replica_groups=mesh['stream'=4,'blk'=8] {'blk'}, use_global_device_ids=true, to_apply=%add.8 | all-reduce | flops 13824 | bytes 55296
  1115.2 9.5 all-reduce.19
  1129.3 6.6 convolution_convert_fusion.5
  1137.5 12.1 fusion.65
  1149.6 52.6 %all-reduce.26.cloned.1.call-done = (bf16[288,1152]{1,0:T(8,128)(2,1)}, bf16[144,3456]{1,0:T(8,128)(2,1)}, bf16[144,1152]{1,0:T(8,128)(2,1)}, bf16[144,4608]{1,0:T(8,128)(2,1)}, bf16[576,1152]{1,0:T(8,128)(2,1)}) async-done(((bf16[288,1152]{1,0:T(8,128)(2,1)}, bf16[144,3456]{1,0:T(8,128)(2,1)}, bf16[144,1152]{1,0:T(8,128)(2,1)}, bf16[144,4608]{1,0:T(8,128)(2,1)}, bf16[576,1152]{1,0:T(8,128)(2,1)}), ...) | async-done | bytes 4644880 | tf_op jit(solution)/shard_map/psum | solution.py:301
  (469 shorter events, 326.5 us)
Async XLA Ops:
  7.3 33.2 %copy-start.16 = (bf16[512,1152]{1,0:T(8,128)(2,1)S(1)}, bf16[512,1152]{1,0:T(8,128)(2,1)}, u32[]{:S(2)}) copy-start(bf16[512,1152]{1,0:T(8,128)(2,1)} %param.22) | copy-start | bytes 3538948
  7.3 59.2 %all-gather.6.cloned.1.call-start = ((), (), s32[]{:S(2)}) async-start(), calls=%async_computation.5 | async-start | bytes 5971968 | tf_op jit(solution)/shard_map/all_gather | solution.py:76
  8.0 33.6 %copy-start.17 = (bf16[512,1152]{1,0:T(8,128)(2,1)S(1)}, bf16[512,1152]{1,0:T(8,128)(2,1)}, u32[]{:S(2)}) copy-start(bf16[512,1152]{1,0:T(8,128)(2,1)} %param.23) | copy-start | bytes 3538948
  8.0 136.9 %all-gather.8.cloned.1.call-start = ((), (), s32[]{:S(2)}) async-start(), calls=%async_computation.6 | async-start | bytes 8957952 | tf_op jit(solution)/shard_map/all_gather | solution.py:80
  8.8 300.9 %all-gather.10.cloned.1.call-start = ((), (), s32[]{:S(2)}) async-start(), calls=%async_computation.7 | async-start | bytes 2985984 | tf_op jit(solution)/shard_map/all_gather | solution.py:81
  9.5 306.9 %all-gather.12.cloned.1.call-start = ((), (), s32[]{:S(2)}) async-start(), calls=%async_computation.8 | async-start | bytes 11943936 | tf_op jit(solution)/shard_map/all_gather | solution.py:85
  10.1 381.1 %all-gather.14.cloned.1.call-start = ((), (), s32[]{:S(2)}) async-start(), calls=%async_computation.9 | async-start | bytes 11943936 | tf_op jit(solution)/shard_map/all_gather | solution.py:87
  40.4 125.0 %copy-start.28 = (f32[1152]{0:T(1024)}, f32[1152]{0:T(1024)S(1)}, u32[]{:S(2)}) copy-start(f32[1152]{0:T(1024)S(1)} %convert_element_type.217) | copy-start | bytes 13828
  40.4 125.0 %copy-start.24 = (f32[1152]{0:T(1024)}, f32[1152]{0:T(1024)S(1)}, u32[]{:S(2)}) copy-start(f32[1152]{0:T(1024)S(1)} %convert_element_type.216) | copy-start | bytes 13828
  73.1 80.7 %copy-start = (f32[512,1152]{1,0:T(8,128)}, f32[512,1152]{1,0:T(8,128)S(1)}, u32[]{:S(2)}) copy-start(f32[512,1152]{1,0:T(8,128)S(1)} %get-tuple-element.320) | copy-start | bytes 7077892
  73.1 80.6 %copy-start.32 = (f32[512]{0:T(512)}, f32[512]{0:T(512)S(1)}, u32[]{:S(2)}) copy-start(f32[512]{0:T(512)S(1)} %broadcast_multiply_fusion.2) | copy-start | bytes 6148
  73.5 80.3 %copy-start.36 = (f32[512]{0:T(512)}, f32[512]{0:T(512)S(1)}, u32[]{:S(2)}) copy-start(f32[512]{0:T(512)S(1)} %multiply_reduce_fusion.6) | copy-start | bytes 6148
  73.5 80.3 %copy-start.46 = (f32[512]{0:T(512)}, f32[512]{0:T(512)S(1)}, u32[]{:S(2)}) copy-start(f32[512]{0:T(512)S(1)} %fusion.68) | copy-start | bytes 6148
  156.3 56.7 %collective-permute-start = (bf16[512,2304]{1,0:T(8,128)(2,1)}, bf16[512,2304]{1,0:T(8,128)(2,1)}, u32[]{:S(2)}, u32[]{:S(2)}) collective-permute-start(bf16[512,2304]{1,0:T(8,128)(2,1)} %slice.46), channel_id=1, source_target_pairs={{0,1},{1,2},{2,3},{3,4},{4,5},{5,6},{6,7},{8,9},{9,10},{10,11},{11... | collective-permute-start | bytes 7077896 | tf_op jit(solution)/shard_map/ppermute | solution.py:16
  158.5 516.8 %all-reduce.24.cloned.1.call-start = ((), (), s32[]{:S(2)}) async-start(), calls=%async_computation.10 | async-start | bytes 1179648 | tf_op jit(solution)/shard_map/psum | solution.py:221
  316.4 74.7 %copy-start.7 = (bf16[512,1152]{1,0:T(8,128)(2,1)S(1)}, bf16[512,1152]{1,0:T(8,128)(2,1)}, u32[]{:S(2)}) copy-start(bf16[512,1152]{1,0:T(8,128)(2,1)} %param.39) | copy-start | bytes 3538948
  391.2 31.9 %copy-start.35 = (f32[512]{0:T(512)S(1)}, f32[512]{0:T(512)}, u32[]{:S(2)}) copy-start(f32[512]{0:T(512)} %copy-done.34) | copy-start | bytes 6148
  391.2 31.9 %copy-start.48 = (f32[512]{0:T(512)S(1)}, f32[512]{0:T(512)}, u32[]{:S(2)}) copy-start(f32[512]{0:T(512)} %fusion.70) | copy-start | bytes 6148
  611.9 37.1 %collective-permute-start.1 = (bf16[512,2304]{0,1:T(8,128)(2,1)}, bf16[512,2304]{0,1:T(8,128)(2,1)}, u32[]{:S(2)}, u32[]{:S(2)}) collective-permute-start(bf16[512,2304]{0,1:T(8,128)(2,1)} %slice.52), channel_id=1, source_target_pairs={{1,0},{2,1},{3,2},{4,3},{5,4},{6,5},{7,6},{9,8},{10,9},{11,10},{12... | collective-permute-start | bytes 7077896 | tf_op jit(solution)/shard_map/ppermute | solution.py:16
  618.8 114.3 %reduce-scatter.10.cloned.1.call-start = ((), (), s32[]{:S(2)}) async-start(), calls=%async_computation.13 | async-start | bytes 2985984 | tf_op jit(solution)/shard_map/reduce_scatter | solution.py:260
  623.3 29.7 %copy-start.18 = (bf16[16,512,72]{1,2,0:T(8,128)(2,1)S(1)}, bf16[16,512,72]{1,2,0:T(8,128)(2,1)}, u32[]{:S(2)}) copy-start(bf16[16,512,72]{1,2,0:T(8,128)(2,1)} %get-tuple-element.111) | copy-start | bytes 3538948
  623.3 29.7 %copy-start.25 = (f32[1152]{0:T(1024)S(1)}, f32[1152]{0:T(1024)}, u32[]{:S(2)}) copy-start(f32[1152]{0:T(1024)} %copy-done.24) | copy-start | bytes 13828
  623.4 29.7 %copy-start.33 = (f32[512]{0:T(512)S(1)}, f32[512]{0:T(512)}, u32[]{:S(2)}) copy-start(f32[512]{0:T(512)} %copy-done.32) | copy-start | bytes 6148
  623.4 150.9 %reduce-scatter.6.cloned.1.call-start = ((), (), s32[]{:S(2)}) async-start(), calls=%async_computation.11 | async-start | bytes 5971968 | tf_op jit(solution)/shard_map/reduce_scatter | solution.py:245
  675.0 185.8 %reduce-scatter.8.cloned.1.call-start = ((), (), s32[]{:S(2)}) async-start(), calls=%async_computation.12 | async-start | bytes 8957952 | tf_op jit(solution)/shard_map/reduce_scatter | solution.py:257
  696.5 275.6 %reduce-scatter.12.cloned.1.call-start = ((), (), s32[]{:S(2)}) async-start(), calls=%async_computation.14 | async-start | bytes 11943936 | tf_op jit(solution)/shard_map/reduce_scatter | solution.py:272
  708.0 375.5 %reduce-scatter.14.cloned.1.call-start = ((), (), s32[]{:S(2)}) async-start(), calls=%async_computation.15 | async-start | bytes 11943936 | tf_op jit(solution)/shard_map/reduce_scatter | solution.py:278
  731.4 352.1 %copy-start.12 = (f32[32,1152]{1,0:T(8,128)S(1)}, f32[32,1152]{1,0:T(8,128)}, u32[]{:S(2)}) copy-start(f32[32,1152]{1,0:T(8,128)} %copy-done.11) | copy-start | bytes 442372
  731.4 352.1 %copy-start.22 = (bf16[32,2304]{0,1:T(8,128)(2,1)S(1)}, bf16[32,2304]{0,1:T(8,128)(2,1)}, u32[]{:S(2)}) copy-start(bf16[32,2304]{0,1:T(8,128)(2,1)} %all-reduce.24.cloned.1.call-done) | copy-start | bytes 442372
  731.4 352.1 %copy-start.45 = (f32[32]{0:T(128)S(1)}, f32[32]{0:T(128)}, u32[]{:S(2)}) copy-start(f32[32]{0:T(128)} %copy-done.44) | copy-start | bytes 388
  731.4 352.1 %copy-start.52 = (f32[32]{0:T(128)S(1)}, f32[32]{0:T(128)}, u32[]{:S(2)}) copy-start(f32[32]{0:T(128)} %copy-done.51) | copy-start | bytes 388
  731.4 470.8 %all-reduce.26.cloned.1.call-start = ((), (), s32[]{:S(2)}) async-start(), calls=%async_computation.16 | async-start | bytes 9289728 | tf_op jit(solution)/shard_map/psum | solution.py:301
  (51 other events, 277.0 us)
Sparse Core Ops, SparseCore 0:
  9.8 56.7 all-gather.5
  68.2 76.7 all-gather.7
  146.6 41.2 all-gather.9
  189.4 101.5 all-gather.11
  292.5 98.6 all-gather.13
  618.9 55.5 all-reduce.23
  677.4 33.7 reduce-scatter.9
  713.5 60.7 reduce-scatter.5
  776.6 84.1 reduce-scatter.7
  863.1 108.9 reduce-scatter.11
  974.4 108.9 reduce-scatter.13
  1088.1 114.0 all-reduce.25
where the time goes:
time: 1230 us; the launch traced here: 1220 us
  waiting for transfers between devices  632 us (51%)
  matrix products  355 us (29%)
  local copies, waits for them, and re-layouts  80.4 us (7%)
  blocking collectives  61.8 us (5%)
  other arithmetic  60.8 us (5%)
  between operations  18.1 us (1%)
    dot_general x54, matrix products, contract_cols(): lax.dot_general(left, right, (((1,), (1,)), ((), ())), preferred_element_...  142 us
    reduce_scatter x1, waiting for transfers between devices, shards(): lax.psum_scatter(grad_down_matrix.astype(jnp.bfloat16), 'blk', scatter_di...  111 us
    reduce_scatter x1, waiting for transfers between devices, shards(): lax.psum_scatter(grad_up_matrix.astype(jnp.bfloat16), 'blk', scatter_dime...  111 us
    dot_general x38, matrix products, contract_rows(): lax.dot_general(left, right, (((0,), (0,)), ((), ())), preferred_element_...  108 us
    reduce_scatter x1, waiting for transfers between devices, shards(): lax.psum_scatter(grad_joint_matrix.astype(jnp.bfloat16), 'blk', scatter_d...  86.6 us
    all_gather x1, waiting for transfers between devices, shards(): lax.all_gather(joint_weight, 'blk', axis=0, tiled=True)  71.5 us
    ppermute x2, waiting for transfers between devices, shifted(): lax.ppermute(value, axis, [(source, source + steps) for source in range(l...  69.7 us
    all_gather x1, waiting for transfers between devices, shards(): lax.all_gather(down_weight, 'blk', axis=0, tiled=True)  61.5 us
  transfers between devices with their start and end apart: 14, of which 10 were waited for; matrix products, arithmetic and copies ran while one was open for 22% of the time, Pallas kernels for 0%

commit v1 on v0

--- a/solution.py
+++ b/solution.py
@@ -3,11 +3,881 @@
 import jax
 import jax.numpy as jnp
 from jax import lax
+from jax.experimental import pallas as pl
+from jax.experimental.pallas import tpu as pltpu
 from jax.sharding import PartitionSpec as P
 
 HEADS = 16
 HEAD = 72
 LEN_MIN = 192
+
+MESH = pl.DeviceIdType.MESH
+ANY = pl.BlockSpec(memory_space=pl.ANY)
+WIDTH = 1152
+PART = 144
+SMALL = (16, 128)
+
+
+class Place:
+    def __init__(self):
+        self.s = lax.axis_index("stream")
+        self.b = lax.axis_index("blk")
+        self.x = lax.rem(self.s, 2)
+        self.y = lax.div(self.s, 2)
+        self.c = lax.rem(self.b, 2)
+        self.zz = lax.div(self.b, 2)
+
+    def flip(self, bit):
+        return 1 - bit
+
+    def other(self, k):
+        low, high = lax.rem(self.zz, 2), lax.div(self.zz, 2)
+        return 2 * (1 - high if k & 2 else high) + (1 - low if k & 1 else low)
+
+    def source(self, k):
+        zz = self.zz
+        table = ((1, 0, 3, 2), (2, 2, 1, 1), (3, 3, 0, 0))[k - 1]
+        return jnp.where(zz < 2, jnp.where(zz == 0, table[0], table[1]), jnp.where(zz == 2, table[2], table[3]))
+
+    def at(self, x=None, y=None, zz=None, c=None):
+        x = self.x if x is None else x
+        y = self.y if y is None else y
+        zz = self.zz if zz is None else zz
+        c = self.c if c is None else c
+        return (2 * y + x, 2 * zz + c)
+
+
+def greet(place):
+    barrier = pltpu.get_barrier_semaphore()
+    near = [
+        place.at(x=1 - place.x),
+        place.at(y=1 - place.y),
+        place.at(c=1 - place.c),
+    ] + [place.at(zz=place.other(k)) for k in (1, 2, 3)]
+    for device in near:
+        pl.semaphore_signal(barrier, inc=1, device_id=device, device_id_type=MESH)
+    pl.semaphore_wait(barrier, len(near))
+
+
+def remote(src, dst, send, recv, device):
+    return pltpu.make_async_remote_copy(
+        src_ref=src, dst_ref=dst, send_sem=send, recv_sem=recv, device_id=device, device_id_type=MESH
+    )
+
+
+def piece(kind, ref, b, x, y):
+    if kind == "cols":
+        return ref.at[b, :, pl.ds(pl.multiple_of((2 * y + x) * WIDTH, 128), WIDTH)]
+    if kind == "rows":
+        return ref.at[b, pl.ds(pl.multiple_of((2 * y + x) * PART, 16), PART)]
+    low, size = (0, 80) if y == 0 else (80, 64)
+    return ref.at[b, pl.ds(pl.multiple_of(x * PART + low, 16), size)]
+
+
+KINDS = ("half", "cols", "cols", "rows")
+
+
+class Gather:
+    SEMS = [pltpu.SemaphoreType.DMA((4, 6, 4, 2)), pltpu.SemaphoreType.DMA((12,)), pltpu.SemaphoreType.DMA((2, 8))]
+
+    def __init__(self, place, shards, outs, scratch):
+        self.place = place
+        self.small_in, self.skip_in, self.joint_in, self.out_in, self.up_in, self.down_in = shards
+        self.small = outs[0]
+        self.outs = outs[1:]
+        self.sems, self.local_sems, self.small_sems = scratch[:3]
+        self.stage = scratch[3:]
+        self.sent = []
+
+    def copy(self, t, x, y, zz, c, stage, k, device):
+        ref = piece(KINDS[t], self.outs[t], 2 * zz + c, x, y)
+        return remote(ref, ref, self.sems.at[t, stage, k, 0], self.sems.at[t, stage, k, 1], device)
+
+    def each_y(self, t, run):
+        if KINDS[t] != "half":
+            run(self.place.y)
+            return
+        for value in (0, 1):
+            pl.when(self.place.y == value)(lambda value=value: run(value))
+
+    STAGE = [
+        pltpu.VMEM((2 * PART, WIDTH), jnp.bfloat16),
+        pltpu.VMEM((PART, 4 * WIDTH), jnp.bfloat16),
+        pltpu.VMEM((PART, 4 * WIDTH), jnp.bfloat16),
+        pltpu.VMEM((4 * PART, WIDTH), jnp.bfloat16),
+    ]
+
+    def locals(self, t):
+        if t == 1:
+            return [
+                (self.joint_in, self.stage[1].at[:, pl.ds(0, 3 * WIDTH)]),
+                (self.out_in, self.stage[1].at[:, pl.ds(3 * WIDTH, WIDTH)]),
+            ]
+        return [({0: self.skip_in, 2: self.up_in, 3: self.down_in}[t], self.stage[t])]
+
+    def own_start(self, t):
+        for i, (src, dst) in enumerate(self.locals(t)):
+            pltpu.make_async_copy(src, dst, self.local_sems.at[2 * t + i]).start()
+
+    def own_keep(self, t):
+        return pltpu.make_async_copy(self.stage[t], self.outs[t].at[self.place.b], self.local_sems.at[8 + t])
+
+    def own_done(self, t):
+        for i, (src, dst) in enumerate(self.locals(t)):
+            pltpu.make_async_copy(src, dst, self.local_sems.at[2 * t + i]).wait()
+        self.own_keep(t).start()
+
+    def own_copy(self, t, c):
+        ref = self.outs[t].at[2 * self.place.zz + c]
+        src = self.stage[t]
+        sems = self.sems.at[t, 4, 0]
+        return remote(src, ref, sems.at[0], sems.at[1], self.place.at(c=1 - self.place.c))
+
+    def small_start(self):
+        p = self.place
+        for i, device in enumerate([p.at(zz=p.other(k)) for k in (1, 2, 3)] + [p.at(c=1 - p.c)]):
+            remote(self.small_in, self.small.at[p.b], self.small_sems.at[0, i], self.small_sems.at[1, i], device).start()
+        pltpu.make_async_copy(self.small_in, self.small.at[p.b], self.small_sems.at[0, 7]).start()
+
+    def small_pass(self):
+        p = self.place
+        for i, k in enumerate((1, 2, 3)):
+            ref = self.small.at[2 * p.other(k) + p.c]
+            remote(ref, ref, self.small_sems.at[0, i], self.small_sems.at[1, i], p.at()).wait_recv()
+            remote(ref, ref, self.small_sems.at[0, 4 + i], self.small_sems.at[1, 4 + i], p.at(c=1 - p.c)).start()
+
+    def small_done(self):
+        p = self.place
+        for i, k in enumerate((0, 1, 2, 3)):
+            ref = self.small.at[2 * p.other(k) + 1 - p.c]
+            remote(ref, ref, self.small_sems.at[0, 3 + i], self.small_sems.at[1, 3 + i], p.at()).wait_recv()
+        for i in range(7):
+            remote(self.small_in, self.small_in, self.small_sems.at[0, i], self.small_sems.at[1, i], p.at()).wait_send()
+        pltpu.make_async_copy(self.small_in, self.small.at[p.b], self.small_sems.at[0, 7]).wait()
+
+    def stage_piece(self, t, y):
+        x = self.place.x
+        q = 2 * y + x
+        if KINDS[t] == "cols":
+            return self.stage[t].at[:, pl.ds(pl.multiple_of(q * WIDTH, 128), WIDTH)]
+        if KINDS[t] == "rows":
+            return self.stage[t].at[pl.ds(pl.multiple_of(q * PART, 16), PART)]
+        low, size = (0, 80) if y == 0 else (80, 64)
+        return self.stage[t].at[pl.ds(pl.multiple_of(x * PART + low, 16), size)]
+
+    def z_copies(self, t, y, zz, start, own=False):
+        p = self.place
+        for step, send in ((1, 0), (-1, 5)):
+            go = (zz <= p.zz) & (p.zz < 3) if step == 1 else (zz >= p.zz) & (p.zz > 0)
+            ref = piece(KINDS[t], self.outs[t], 2 * zz + p.c, p.x, y)
+
+            @pl.when(go)
+            def _():
+                copy = remote(self.stage_piece(t, y) if own else ref, ref, self.sems.at[t, send, zz, 0], self.sems.at[t, 0, zz, 1], p.at(zz=p.zz + step))
+                copy.start() if start else copy.wait_send()
+
+    def z_start(self, t):
+        p = self.place
+        self.each_y(t, lambda y: self.z_copies(t, y, p.zz, True, True))
+        self.own_copy(t, p.c).start()
+
+    def z_done(self, t, k):
+        p = self.place
+        zz = p.source(k)
+
+        def run(y):
+            self.copy(t, p.x, y, zz, p.c, 0, zz, p.at()).wait_recv()
+            self.copy(t, p.x, y, zz, p.c, 1, k, p.at(x=1 - p.x)).start()
+            self.copy(t, p.x, y, zz, p.c, 2, k, p.at(y=1 - p.y)).start()
+            self.z_copies(t, y, zz, True)
+
+        self.each_y(t, run)
+
+    def by_x(self, t, k):
+        return k == 1 or (k == 2 and t % 2 == 0)
+
+    def xy_done(self, t, k):
+        p = self.place
+
+        def run(y):
+            zz = p.source(k)
+            self.copy(t, 1 - p.x, y, zz, p.c, 1, k, p.at()).wait_recv()
+            if self.by_x(t, k):
+                self.copy(t, 1 - p.x, y, zz, p.c, 3, k, p.at(y=1 - p.y)).start()
+            self.copy(t, p.x, 1 - y, zz, p.c, 2, k, p.at()).wait_recv()
+            if not self.by_x(t, k):
+                self.copy(t, p.x, 1 - y, zz, p.c, 3, k, p.at(x=1 - p.x)).start()
+
+        self.each_y(t, run)
+
+    def diag_done(self, t, k):
+        p = self.place
+
+        def run(y):
+            zz = p.source(k)
+            self.copy(t, 1 - p.x, 1 - y, zz, p.c, 3, k, p.at()).wait_recv()
+
+        self.each_y(t, run)
+        self.pair_copy(t, k, p.c).start()
+
+    def pair_copy(self, t, k, c):
+        ref = self.outs[t].at[2 * self.place.source(k) + c]
+        sems = self.sems.at[t, 4, k]
+        return remote(ref, ref, sems.at[0], sems.at[1], self.place.at(c=1 - self.place.c))
+
+    def ready(self, t):
+        p = self.place
+        self.own_copy(t, 1 - p.c).wait_recv()
+        for k in (1, 2, 3):
+            self.pair_copy(t, k, 1 - p.c).wait_recv()
+
+    def all_sent(self, t):
+        p = self.place
+        self.own_copy(t, p.c).wait_send()
+        self.own_keep(t).wait()
+
+        def run(y):
+            self.z_copies(t, y, p.zz, False, True)
+            for k in (1, 2, 3):
+                zz = p.source(k)
+                self.z_copies(t, y, zz, False)
+                self.copy(t, p.x, y, zz, p.c, 1, k, p.at()).wait_send()
+                self.copy(t, p.x, y, zz, p.c, 2, k, p.at()).wait_send()
+                if self.by_x(t, k):
+                    self.copy(t, 1 - p.x, y, zz, p.c, 3, k, p.at()).wait_send()
+                else:
+                    self.copy(t, p.x, 1 - y, zz, p.c, 3, k, p.at()).wait_send()
+
+        self.each_y(t, run)
+        for k in (1, 2, 3):
+            self.pair_copy(t, k, p.c).wait_send()
+
+
+def gather_kernel(*refs):
+    shards, outs, scratch = refs[:6], refs[6:11], refs[11:]
+    place = Place()
+    g = Gather(place, shards, outs, scratch)
+    for t in range(4):
+        g.own_start(t)
+    greet(place)
+    g.small_start()
+    g.own_done(0)
+    g.z_start(0)
+    g.small_pass()
+    for t in range(4):
+        for k in (1, 2, 3):
+            g.z_done(t, k)
+        if t + 1 < 4:
+            g.own_done(t + 1)
+            g.z_start(t + 1)
+        if t > 0:
+            for k in (1, 2, 3):
+                g.diag_done(t - 1, k)
+        for k in (1, 2, 3):
+            g.xy_done(t, k)
+    for k in (1, 2, 3):
+        g.diag_done(3, k)
+    g.small_done()
+    for t in range(4):
+        g.ready(t)
+        g.all_sent(t)
+
+
+def gather_weights(small, skip, joint, out, up, down):
+    bf16 = jnp.bfloat16
+    return pl.pallas_call(
+        gather_kernel,
+        out_shape=[
+            jax.ShapeDtypeStruct((8, *SMALL), bf16),
+            jax.ShapeDtypeStruct((8, 2 * PART, WIDTH), bf16),
+            jax.ShapeDtypeStruct((8, PART, 4 * WIDTH), bf16),
+            jax.ShapeDtypeStruct((8, PART, 4 * WIDTH), bf16),
+            jax.ShapeDtypeStruct((8, 4 * PART, WIDTH), bf16),
+        ],
+        in_specs=[ANY] * 6,
+        out_specs=[ANY] * 5,
+        scratch_shapes=Gather.SEMS + Gather.STAGE,
+        compiler_params=pltpu.CompilerParams(collective_id=0, has_side_effects=True),
+    )(small, skip, joint, out, up, down)
+
+
+def add_units(out, *ins):
+    @pl.loop(0, out.shape[0] // 16)
+    def _(i):
+        rows = pl.ds(pl.multiple_of(i * 16, 16), 16)
+        total = ins[0][rows].astype(jnp.float32)
+        for ref in ins[1:]:
+            total += ref[rows].astype(jnp.float32)
+        out[rows] = total.astype(out.dtype)
+
+
+SIZES = (80, PART, PART, PART)
+
+
+class Reduce:
+    SEMS = [
+        pltpu.SemaphoreType.DMA((4, 4, 2, 3)),
+        pltpu.SemaphoreType.DMA((4, 4, 2)),
+        pltpu.SemaphoreType.DMA((4, 4, 2)),
+        pltpu.SemaphoreType.DMA((4, 4, 2)),
+    ]
+    BUFFERS = [
+        pltpu.VMEM(lead + (size, WIDTH), jnp.bfloat16)
+        for size in SIZES
+        for lead in ((4, 2), (4, 2), (4,), (4,), ())
+    ]
+
+    def __init__(self, place, parts, outs, scratch):
+        self.place, self.parts, self.outs = place, parts, outs
+        self.sem1, self.sem2, self.sem3, self.sem4 = scratch[:4]
+        bufs = scratch[4:]
+        self.stage, self.land1, self.land2, self.land3, self.fin = (
+            [bufs[5 * t + i] for t in range(4)] for i in range(5)
+        )
+
+    def piece(self, t, zz, x, y):
+        ref = self.parts[t]
+        if KINDS[t] == "cols":
+            return ref.at[zz, :, pl.ds(pl.multiple_of((2 * y + x) * WIDTH, 128), WIDTH)]
+        if KINDS[t] == "rows":
+            return ref.at[zz, pl.ds(pl.multiple_of((2 * y + x) * PART, 16), PART)]
+        return ref.at[zz, pl.ds(pl.multiple_of(x * PART + 64 * y, 16), 80)]
+
+    def first(self, t, zz, j):
+        p = self.place
+        if zz < 2:
+            src, device = self.piece(t, zz, 1 - p.x, j), p.at(x=1 - p.x)
+        else:
+            src, device = self.piece(t, zz, j, 1 - p.y), p.at(y=1 - p.y)
+        sems = self.sem1.at[t, zz, j]
+        return remote(src, self.land1[t].at[zz, j], sems.at[0], sems.at[1], device)
+
+    def load(self, t, zz, j):
+        p = self.place
+        src = self.piece(t, zz, p.x, j) if zz < 2 else self.piece(t, zz, j, p.y)
+        return pltpu.make_async_copy(src, self.stage[t].at[zz, j], self.sem1.at[t, zz, j, 2])
+
+    def start(self, t):
+        for zz in (0, 2, 1, 3):
+            for j in (0, 1):
+                self.first(t, zz, j).start()
+                self.load(t, zz, j).start()
+
+    def second(self, t, zz):
+        p = self.place
+        keep = p.y if zz < 2 else p.x
+        device = p.at(y=1 - p.y) if zz < 2 else p.at(x=1 - p.x)
+        sems = self.sem2.at[t, zz]
+        return remote(self.stage[t].at[zz, 1 - keep], self.land2[t].at[zz], sems.at[0], sems.at[1], device)
+
+    def pass_on(self, t):
+        p = self.place
+        for zz in (0, 2, 1, 3):
+            keep = p.y if zz < 2 else p.x
+            for j in (0, 1):
+                self.load(t, zz, j).wait()
+                self.first(t, zz, j).wait_recv()
+            mine = self.stage[t].at[zz, 1 - keep]
+            add_units(mine, mine, self.land1[t].at[zz, 1 - keep])
+            self.second(t, zz).start()
+
+    def third(self, t, zz, slot):
+        p = self.place
+        keep = p.y if zz < 2 else p.x
+        return remote(
+            self.stage[t].at[zz, keep], self.land3[t].at[slot], self.sem3.at[t, zz, 0], self.sem3.at[t, slot, 1],
+            p.at(zz=zz),
+        )
+
+    def to_chip(self, t):
+        p = self.place
+        for zz in (0, 2, 1, 3):
+            keep = p.y if zz < 2 else p.x
+            self.second(t, zz).wait_recv()
+            mine = self.stage[t].at[zz, keep]
+            add_units(mine, mine, self.land1[t].at[zz, keep], self.land2[t].at[zz])
+
+            @pl.when(zz != p.zz)
+            def _():
+                self.third(t, zz, p.zz).start()
+
+            @pl.when(zz == p.zz)
+            def _():
+                add_units(self.fin[t], mine)
+
+    def share(self, t, k):
+        p = self.place
+        x = 1 - p.x if k & 1 else p.x
+        y = 1 - p.y if k & 2 else p.y
+        return p.at(x=x, y=y), self.sem4.at[t, k]
+
+    def result(self, t, x, y):
+        ref = self.outs[t]
+        if KINDS[t] == "cols":
+            return ref.at[:, pl.ds(pl.multiple_of((2 * y + x) * WIDTH, 128), WIDTH)]
+        if KINDS[t] == "rows":
+            return ref.at[pl.ds(pl.multiple_of((2 * y + x) * PART, 16), PART)]
+        low, size = (0, 80) if y == 0 else (80, 64)
+        return ref.at[pl.ds(pl.multiple_of(x * PART + low, 16), size)]
+
+    def fin_part(self, t, y):
+        if KINDS[t] != "half":
+            return self.fin[t]
+        return self.fin[t] if y == 0 else self.fin[t].at[pl.ds(16, 64)]
+
+    def each_y(self, t, run):
+        if KINDS[t] != "half":
+            run(self.place.y)
+            return
+        for value in (0, 1):
+            pl.when(self.place.y == value)(lambda value=value: run(value))
+
+    def spread(self, t, start):
+        p = self.place
+
+        def run(y):
+            src, dst = self.fin_part(t, y), self.result(t, p.x, y)
+            for k in (1, 2, 3):
+                device, sems = self.share(t, k)
+                copy = remote(src, dst, sems.at[0], sems.at[1], device)
+                copy.start() if start else copy.wait_send()
+            keep = pltpu.make_async_copy(src, dst, self.sem4.at[t, 0, 0])
+            keep.start() if start else keep.wait()
+
+        self.each_y(t, run)
+
+    def finish(self, t):
+        p = self.place
+        for k in (1, 2, 3):
+            ref = self.land3[t].at[p.other(k)]
+            remote(ref, ref, self.sem3.at[t, p.zz, 0], self.sem3.at[t, p.other(k), 1], p.at()).wait_recv()
+        add_units(self.fin[t], self.fin[t], *[self.land3[t].at[p.other(k)] for k in (1, 2, 3)])
+        self.spread(t, True)
+
+    def done(self, t):
+        p = self.place
+        for zz in range(4):
+            for j in (0, 1):
+                self.first(t, zz, j).wait_send()
+            self.second(t, zz).wait_send()
+
+            @pl.when(zz != p.zz)
+            def _():
+                self.third(t, zz, p.zz).wait_send()
+
+        self.spread(t, False)
+
+        def run(y):
+            for k in (1, 2, 3):
+                ref = self.result(t, 1 - p.x if k & 1 else p.x, 1 - y if k & 2 else y)
+                sems = self.sem4.at[t, k]
+                remote(ref, ref, sems.at[0], sems.at[1], p.at()).wait_recv()
+
+        self.each_y(t, run)
+
+
+class Little:
+    SCRATCH = [
+        pltpu.VMEM((8, *SMALL), jnp.float32),
+        pltpu.VMEM((4, *SMALL), jnp.float32),
+        pltpu.VMEM((4, *SMALL), jnp.float32),
+        pltpu.VMEM((4, *SMALL), jnp.float32),
+        pltpu.VMEM((4, *SMALL), jnp.float32),
+        pltpu.VMEM((4, *SMALL), jnp.float32),
+        pltpu.VMEM(SMALL, jnp.float32),
+        pltpu.VMEM((32, WIDTH), jnp.float32),
+        pltpu.VMEM((32, WIDTH), jnp.float32),
+        pltpu.VMEM((32, WIDTH), jnp.float32),
+        pltpu.VMEM((4, 32, WIDTH), jnp.float32),
+        pltpu.VMEM((32, WIDTH), jnp.bfloat16),
+        pltpu.SemaphoreType.DMA((16, 2)),
+    ]
+
+    def __init__(self, place, small, cond, small_out, cond_out, scratch):
+        self.place, self.ins, self.outs = place, (small, cond), (small_out, cond_out)
+        self.part, self.pair, self.x_in, self.sum1, self.y_in, self.z_in, self.total = scratch[:7]
+        self.mine, self.cond_pair, self.cond_sum, self.cond_in, self.cond_out = scratch[7:12]
+        self.sems = scratch[12]
+
+    def copy(self, i, src, dst, device, j=None):
+        return remote(src, dst, self.sems.at[i, 0], self.sems.at[i if j is None else j, 1], device)
+
+    def load(self):
+        for i, (src, dst) in enumerate(((self.ins[0], self.part), (self.ins[1], self.mine))):
+            pltpu.make_async_copy(src, dst, self.sems.at[14 + i, 0]).start()
+        for i, (src, dst) in enumerate(((self.ins[0], self.part), (self.ins[1], self.mine))):
+            pltpu.make_async_copy(src, dst, self.sems.at[14 + i, 0]).wait()
+
+    def small_pair(self, zz):
+        p = self.place
+        return self.copy(zz, self.part.at[2 * zz + 1 - p.c], self.pair.at[zz], p.at(c=1 - p.c))
+
+    def run_pair(self):
+        p = self.place
+        for zz in range(4):
+            self.small_pair(zz).start()
+        cond = self.copy(4, self.mine, self.cond_pair, p.at(c=1 - p.c))
+        cond.start()
+        for zz in range(4):
+            self.small_pair(zz).wait()
+            self.pair[zz] += self.part[2 * zz + p.c]
+        cond.wait()
+        self.cond_sum[...] = self.mine[...] + self.cond_pair[...]
+        self.copy(5, self.pair, self.x_in, p.at(x=1 - p.x)).start()
+        for k in (1, 2, 3):
+            self.copy(6 + k, self.cond_sum, self.cond_in.at[p.zz], p.at(zz=p.other(k))).start()
+        self.cond_in[p.zz] = self.cond_sum[...]
+
+    def run_x(self):
+        p = self.place
+        self.copy(5, self.pair, self.x_in, p.at(x=1 - p.x)).wait()
+        self.sum1[...] = self.pair[...] + self.x_in[...]
+        self.copy(6, self.sum1, self.y_in, p.at(y=1 - p.y)).start()
+
+    def run_y(self):
+        p = self.place
+        self.copy(6, self.sum1, self.y_in, p.at(y=1 - p.y)).wait()
+        self.sum1[...] += self.y_in[...]
+        for k in (1, 2, 3):
+            self.copy(9 + k, self.sum1.at[p.other(k)], self.z_in.at[p.zz], p.at(zz=p.other(k))).start()
+        self.z_in[p.zz] = self.sum1[p.zz]
+
+    def run_z(self):
+        p = self.place
+        for k in (1, 2, 3):
+            self.copy(9 + k, self.sum1.at[p.other(k)], self.z_in.at[p.zz], p.at(zz=p.other(k))).wait()
+            self.copy(6 + k, self.cond_sum, self.cond_in.at[p.zz], p.at(zz=p.other(k))).wait()
+        self.total[...] = (self.z_in[0] + self.z_in[1]) + (self.z_in[2] + self.z_in[3])
+        cond = (self.cond_in[0] + self.cond_in[1]) + (self.cond_in[2] + self.cond_in[3])
+        self.cond_out[...] = cond.astype(jnp.bfloat16)
+        pairs = ((self.total, self.outs[0]), (self.cond_out, self.outs[1]))
+        for i, (src, dst) in enumerate(pairs):
+            pltpu.make_async_copy(src, dst, self.sems.at[14 + i, 0]).start()
+        for i, (src, dst) in enumerate(pairs):
+            pltpu.make_async_copy(src, dst, self.sems.at[14 + i, 0]).wait()
+
+
+N_RED = len(Reduce.SEMS) + len(Reduce.BUFFERS)
+
+
+def reduce_kernel(*refs):
+    parts, small, cond, outs, small_out, cond_out = refs[:4], refs[4], refs[5], refs[6:10], refs[10], refs[11]
+    scratch = refs[12:]
+    place = Place()
+    r = Reduce(place, parts, outs, scratch[:N_RED])
+    little = Little(place, small, cond, small_out, cond_out, scratch[N_RED:])
+    greet(place)
+    order = (3, 2, 1, 0)
+    r.start(order[0])
+    little.load()
+    little.run_pair()
+    little.run_x()
+    little.run_y()
+    for i, t in enumerate(order):
+        r.pass_on(t)
+        if i < 3:
+            r.start(order[i + 1])
+        if i > 0:
+            r.finish(order[i - 1])
+        r.to_chip(t)
+    r.finish(order[3])
+    little.run_z()
+    for t in order:
+        r.done(t)
+
+
+def reduce_grads(parts, small, cond):
+    bf16 = jnp.bfloat16
+    return pl.pallas_call(
+        reduce_kernel,
+        out_shape=[
+            jax.ShapeDtypeStruct((2 * PART, WIDTH), bf16),
+            jax.ShapeDtypeStruct((PART, 4 * WIDTH), bf16),
+            jax.ShapeDtypeStruct((PART, 4 * WIDTH), bf16),
+            jax.ShapeDtypeStruct((4 * PART, WIDTH), bf16),
+            jax.ShapeDtypeStruct(SMALL, jnp.float32),
+            jax.ShapeDtypeStruct((32, WIDTH), bf16),
+        ],
+        in_specs=[ANY] * 6,
+        out_specs=[ANY] * 6,
+        scratch_shapes=Reduce.SEMS + Reduce.BUFFERS + Little.SCRATCH,
+        compiler_params=pltpu.CompilerParams(collective_id=1, has_side_effects=True, vmem_limit_bytes=58 << 20),
+    )(*parts, small, cond)
+
+
+HALO = 320
+COND = 32
+TILES = ((0, 0), (256, 256))
+LOG2E = 1.4426950408889634
+
+
+def nt(a, b):
+    return lax.dot_general(a, b, (((1,), (1,)), ((), ())), preferred_element_type=jnp.float32)
+
+
+def tn(a, b):
+    return lax.dot_general(a, b, (((0,), (0,)), ((), ())), preferred_element_type=jnp.float32)
+
+
+def nn(a, b):
+    return jnp.dot(a, b, preferred_element_type=jnp.float32)
+
+
+def make_bias(seg_q, seg_k, bias):
+    bias[...] = jnp.where(seg_q[...] == seg_k[...], 0.0, -1e30)
+
+
+def head(h):
+    return slice(HEAD * h, HEAD * (h + 1))
+
+
+def attend_kernel(query, pairs, seg_q, seg_k, attended, logsum, heads_q, heads_k, heads_v, heads_o, bias):
+    make_bias(seg_q, seg_k, bias)
+    for h in range(HEADS):
+        heads_q[h] = query[:, head(h)]
+        heads_k[h] = pairs[:, head(h)]
+        heads_v[h] = pairs[:, HEADS * HEAD + HEAD * h : HEADS * HEAD + HEAD * (h + 1)]
+
+    @pl.loop(0, HEADS)
+    def _(h):
+        for row, low in TILES:
+            rows, keys = pl.ds(row, 256), pl.ds(low, HALO + 512 + COND - low)
+            scores = nt(heads_q[h, rows], heads_k[h, keys]) * (HEAD**-0.5 * LOG2E) + bias[rows, keys]
+            top = jnp.max(scores, axis=1, keepdims=True)
+            expo = jnp.exp2(scores - top)
+            total = jnp.sum(expo, axis=1, keepdims=True)
+            mixed = nn(expo.astype(jnp.bfloat16), heads_v[h, keys])
+            heads_o[h, rows] = (mixed / total).astype(jnp.bfloat16)
+            logsum[h, rows] = top + jnp.log2(total)
+
+    for h in range(HEADS):
+        attended[:, head(h)] = heads_o[h]
+
+
+def vmem(shape, dtype):
+    return pltpu.VMEM(shape, dtype)
+
+
+def attend(query, pairs, seg_q, seg_k):
+    rows, keys = query.shape[0], pairs.shape[0]
+    bf16 = jnp.bfloat16
+    return pl.pallas_call(
+        attend_kernel,
+        out_shape=[
+            jax.ShapeDtypeStruct((rows, HEADS * HEAD), bf16),
+            jax.ShapeDtypeStruct((HEADS, rows, 1), jnp.float32),
+        ],
+        scratch_shapes=[
+            vmem((HEADS, rows, HEAD), bf16),
+            vmem((HEADS, keys, HEAD), bf16),
+            vmem((HEADS, keys, HEAD), bf16),
+            vmem((HEADS, rows, HEAD), bf16),
+            vmem((rows, keys), jnp.float32),
+        ],
+        compiler_params=pltpu.CompilerParams(vmem_limit_bytes=50 << 20),
+    )(query, pairs, seg_q, seg_k)
+
+
+def attend_back_kernel(
+    query, pairs, attended, grad, logsum, seg_q, seg_k, d_query, d_pairs,
+    heads_q, heads_k, heads_v, heads_o, heads_g, heads_dk, heads_dv, sum_k, sum_v, bias,
+):
+    make_bias(seg_q, seg_k, bias)
+    for h in range(HEADS):
+        heads_q[h] = query[:, head(h)]
+        heads_k[h] = pairs[:, head(h)]
+        heads_v[h] = pairs[:, HEADS * HEAD + HEAD * h : HEADS * HEAD + HEAD * (h + 1)]
+        heads_o[h] = attended[:, head(h)]
+        heads_g[h] = grad[:, head(h)]
+    scale = HEAD**-0.5
+
+    @pl.loop(0, HEADS)
+    def _(h):
+        for row, low in TILES:
+            rows, keys = pl.ds(row, 256), pl.ds(low, HALO + 512 + COND - low)
+            q, k, v, g = heads_q[h, rows], heads_k[h, keys], heads_v[h, keys], heads_g[h, rows]
+            scores = nt(q, k) * (scale * LOG2E) + bias[rows, keys]
+            probs = jnp.exp2(scores - logsum[h, rows])
+            d_probs = nt(g, v)
+            inner = jnp.sum(g.astype(jnp.float32) * heads_o[h, rows].astype(jnp.float32), axis=1, keepdims=True)
+            d_scores = (probs * (d_probs - inner)).astype(jnp.bfloat16)
+            d_k, d_v = tn(d_scores, q), tn(probs.astype(jnp.bfloat16), g)
+            if row == 0:
+                sum_k[...] = d_k
+                sum_v[...] = d_v
+            else:
+                sum_k[keys] += d_k
+                sum_v[keys] += d_v
+            heads_o[h, rows] = (nn(d_scores, k) * scale).astype(jnp.bfloat16)
+        heads_dk[h] = (sum_k[...] * scale).astype(jnp.bfloat16)
+        heads_dv[h] = sum_v[...].astype(jnp.bfloat16)
+
+    for h in range(HEADS):
+        d_query[:, head(h)] = heads_o[h]
+        d_pairs[:, head(h)] = heads_dk[h]
+        d_pairs[:, HEADS * HEAD + HEAD * h : HEADS * HEAD + HEAD * (h + 1)] = heads_dv[h]
+
+
+def attend_back(query, pairs, attended, grad, logsum, seg_q, seg_k):
+    rows, keys = query.shape[0], pairs.shape[0]
+    bf16 = jnp.bfloat16
+    small, large = (HEADS, rows, HEAD), (HEADS, keys, HEAD)
+    return pl.pallas_call(
+        attend_back_kernel,
+        out_shape=[
+            jax.ShapeDtypeStruct((rows, HEADS * HEAD), bf16),
+            jax.ShapeDtypeStruct((keys, 2 * HEADS * HEAD), bf16),
+        ],
+        scratch_shapes=[
+            vmem(small, bf16), vmem(large, bf16), vmem(large, bf16), vmem(small, bf16), vmem(small, bf16),
+            vmem(large, bf16), vmem(large, bf16),
+            vmem((keys, HEAD), jnp.float32), vmem((keys, HEAD), jnp.float32),
+            vmem((rows, keys), jnp.float32),
+        ],
+        compiler_params=pltpu.CompilerParams(vmem_limit_bytes=58 << 20),
+    )(query, pairs, attended, grad, logsum, seg_q, seg_k)
+
+
+def item_ends(extra_length):
+    lengths = extra_length[0] + (LEN_MIN - 1)
+    count = lengths.shape[0]
+    upto = lax.iota(jnp.int32, count)[None, :] <= lax.iota(jnp.int32, count)[:, None]
+    return jnp.sum(jnp.where(upto, lengths[None, :], 0), axis=1)
+
+
+def norm_parts(values):
+    center = values - jnp.mean(values, axis=-1, keepdims=True)
+    spread = jnp.mean(center * center, axis=-1, keepdims=True)
+    rstd = lax.rsqrt(spread + 1e-05)
+    return center * rstd, rstd
+
+
+def norm_back(unit, rstd, gain, grad):
+    scaled = grad * gain
+    first = jnp.mean(scaled, axis=-1, keepdims=True)
+    second = jnp.mean(scaled * unit, axis=-1, keepdims=True)
+    return rstd * (scaled - first - unit * second), jnp.sum(grad * unit, axis=0), jnp.sum(grad, axis=0)
+
+
+def quick(
+    latents, skip_input, cond_tokens, extra_length, skip_weight, skip_bias, first_gain, first_shift, joint_weight,
+    out_weight, out_bias, second_gain, second_shift, up_weight, up_bias, down_weight, down_bias, cotangent,
+):
+    f32, bf16 = jnp.float32, jnp.bfloat16
+    vectors = (skip_bias, first_gain, first_shift, out_bias, second_gain, second_shift, down_bias, up_bias)
+    packed = jnp.concatenate(vectors + (jnp.zeros((SMALL[0] * SMALL[1] - 11 * PART,), bf16),)).reshape(SMALL)
+    small, skip_all, joint_all, up_all, down_all = gather_weights(
+        packed, skip_weight, joint_weight, out_weight, up_weight, down_weight
+    )
+    small = small.reshape(8, SMALL[0] * SMALL[1])
+    skip_offset, gain_first, shift_first, out_offset, gain_second, shift_second, down_offset = (
+        v.reshape(WIDTH).astype(f32) for v in jnp.split(small[:, : 7 * PART], 7, axis=1)
+    )
+    up_offset = small[:, 7 * PART : 11 * PART].reshape(4 * WIDTH).astype(f32)
+    skip_matrix = skip_all.reshape(2 * WIDTH, WIDTH)
+    joint_out = joint_all.reshape(WIDTH, 4 * WIDTH)
+    joint_matrix, out_matrix = joint_out[:, : 3 * WIDTH], joint_out[:, 3 * WIDTH :]
+    up_matrix = up_all.reshape(WIDTH, 4 * WIDTH)
+    down_matrix = down_all.reshape(4 * WIDTH, WIDTH)
+
+    rows, width = latents.shape
+    here = lax.axis_index("blk")
+    ends = item_ends(extra_length)
+    places = here * rows + lax.iota(jnp.int32, HALO + rows) - HALO
+    items = jnp.where(places >= 0, jnp.sum((ends[None, :] <= places[:, None]).astype(jnp.int32), axis=1), -1)
+    seg_q = items[HALO:, None]
+    seg_k = jnp.concatenate([items, lax.iota(jnp.int32, COND) // 2])[None, :]
+
+    base = nn(latents, skip_matrix[:width]) + nn(skip_input, skip_matrix[width:]) + skip_offset
+    first_unit, first_rstd = norm_parts(base)
+    first_in = (first_unit * gain_first + shift_first).astype(bf16)
+    triple = nn(first_in, joint_matrix).astype(bf16)
+    cond_flat = cond_tokens.reshape(-1, width).astype(f32)
+    cond_unit, cond_rstd = norm_parts(cond_flat)
+    cond_in = (cond_unit * gain_first + shift_first).astype(bf16)
+    cond_pair = nn(cond_in, joint_matrix[:, width:]).astype(bf16)
+    halo = lax.ppermute(triple[rows - HALO :, width:], "blk", [(i, i + 1) for i in range(7)])
+    query, pairs = triple[:, :width], jnp.concatenate([halo, triple[:, width:], cond_pair], 0)
+    attended, logsum = attend(query, pairs, seg_q, seg_k)
+    middle = base + nn(attended, out_matrix) + out_offset
+    second_unit, second_rstd = norm_parts(middle)
+    second_in = (second_unit * gain_second + shift_second).astype(bf16)
+    before = nn(second_in, up_matrix) + up_offset
+    inside = 0.5 * (1.0 + lax.erf(before * 2**-0.5))
+    slope = (inside + before * jnp.exp(-0.5 * before * before) * (2 * jnp.pi) ** -0.5).astype(bf16)
+    hidden = (before * inside).astype(bf16)
+    hidden, slope = lax.optimization_barrier((hidden, slope))
+    output = middle + nn(hidden, down_matrix) + down_offset
+
+    core = lax.rem(here, 2)
+
+    def chip(grad):
+        halves = grad.astype(bf16).reshape(4, 2, -1, grad.shape[1])
+        mine = lax.dynamic_index_in_dim(halves, core, 1, keepdims=False)
+        other = lax.dynamic_index_in_dim(halves, 1 - core, 1, keepdims=False)
+        received = lax.ppermute(other, "blk", [(i, i ^ 1) for i in range(8)])
+        return (mine.astype(f32) + received.astype(f32)).astype(bf16)
+
+    g = cotangent.astype(f32)
+    sum_down = jnp.sum(g, axis=0)
+    part_down = chip(tn(hidden, cotangent))
+    d_before = (nt(cotangent, down_matrix) * slope.astype(f32)).astype(bf16)
+    sum_up = jnp.sum(d_before.astype(f32), axis=0)
+    part_up = chip(tn(second_in, d_before))
+    d_second = nt(d_before, up_matrix)
+    d_norm, sum_gain_second, sum_shift_second = norm_back(second_unit, second_rstd, gain_second, d_second)
+    d_middle = g + d_norm
+    d_branch = d_middle.astype(bf16)
+    sum_out = jnp.sum(d_branch.astype(f32), axis=0)
+    part_out = tn(attended, d_branch)
+    d_attended = nt(d_branch, out_matrix).astype(bf16)
+    d_query, d_pairs = attend_back(query, pairs, attended, d_attended, logsum, seg_q, seg_k)
+    returned = lax.ppermute(d_pairs[:HALO], "blk", [(i + 1, i) for i in range(7)])
+    own = d_pairs[HALO : HALO + rows].astype(f32) + jnp.pad(returned.astype(f32), ((rows - HALO, 0), (0, 0)))
+    d_triple = jnp.concatenate([d_query, own.astype(bf16)], 1)
+    d_cond = d_pairs[HALO + rows :]
+    cond_rows = jnp.concatenate([jnp.zeros((COND, width), bf16), d_cond], 1)
+    part_joint = tn(first_in, d_triple) + tn(cond_in, cond_rows)
+    part_joint_out = chip(jnp.concatenate([part_joint, part_out], 1))
+    d_first = nt(d_triple, joint_matrix)
+    d_norm, sum_gain_first, sum_shift_first = norm_back(first_unit, first_rstd, gain_first, d_first)
+    d_cond_in = nt(d_cond, joint_matrix[:, width:])
+    d_cond_flat, sum_gain_cond, sum_shift_cond = norm_back(cond_unit, cond_rstd, gain_first, d_cond_in)
+    d_base = (d_middle + d_norm).astype(bf16)
+    sum_skip = jnp.sum(d_base.astype(f32), axis=0)
+    part_skip = chip(jnp.concatenate([tn(latents, d_base), tn(skip_input, d_base)], 0))
+    d_joined = nt(d_base, skip_matrix).astype(bf16)
+
+    sums = (
+        sum_skip, sum_gain_first + sum_gain_cond, sum_shift_first + sum_shift_cond, sum_out, sum_gain_second,
+        sum_shift_second, sum_down, sum_up,
+    )
+    flat = jnp.concatenate([v.reshape(8, -1) for v in sums], axis=1)
+    flat = jnp.pad(flat, ((0, 0), (0, SMALL[0] * SMALL[1] - flat.shape[1]))).reshape(8, *SMALL)
+    skip_sum, joint_out_sum, up_sum, down_sum, small_sum, cond_sum = reduce_grads(
+        (part_skip, part_joint_out, part_up, part_down), flat, d_cond_flat
+    )
+    small_sum = small_sum.reshape(-1)
+    v = jnp.split(small_sum[: 7 * PART], 7)
+    return (
+        output.astype(bf16),
+        d_joined[:, :width],
+        d_joined[:, width:],
+        cond_sum.reshape(cond_tokens.shape),
+        skip_sum.astype(f32),
+        v[0],
+        v[1],
+        v[2],
+        joint_out_sum[:, : 3 * WIDTH].astype(f32),
+        joint_out_sum[:, 3 * WIDTH :].astype(f32),
+        v[3],
+        v[4],
+        v[5],
+        up_sum.astype(f32),
+        small_sum[7 * PART : 11 * PART],
+        down_sum.astype(f32),
+        v[6],
+    )
 
 
 def shifted(value, axis, steps):
@@ -52,7 +922,7 @@
     return jnp.where(allowed, scores, -1e30)
 
 
-def shards(
+def plain(
     latents,
     skip_input,
     cond_tokens,
@@ -120,7 +990,7 @@
         cond_in, joint_matrix[:, width:], preferred_element_type=jnp.float32
     ).astype(jnp.bfloat16)
     pairs = jnp.concatenate([pair_left, pair_here, cond_pair], 0)
-    ends = jnp.cumsum(extra_length[0] + (LEN_MIN - 1))
+    ends = item_ends(extra_length)
     here = lax.axis_index("blk")
     places = here * rows + lax.iota(jnp.int32, rows)
     seg_here = segment_ids(ends, places)
@@ -354,8 +1224,9 @@
         P("blk"),
         P(("stream", "blk"), None),
     )
+    fits = mesh.shape["stream"] == 4 and mesh.shape["blk"] == 8
     return jax.shard_map(
-        shards,
+        quick if fits else plain,
         mesh=mesh,
         in_specs=placed,
         out_specs=(

time: 1230 us -> 695 us (0.57)
  waiting for transfers between devices: 632 us -> 6.95 us
  Pallas kernels: 0 us -> 415 us
  matrix products: 355 us -> 134 us
  blocking collectives: 61.8 us -> 0 us
  local copies, waits for them, and re-layouts: 80.4 us -> 62 us
  between operations: 18.1 us -> 2.32 us
    pallas_call x0 -> x4, Pallas kernels: none -> 415 us  [the longest x1 215 us: reduce_grads(): pl.pallas_call(reduce_kernel, out_shape=[jax.ShapeDtypeStruct((2 * PART,...]
    reduce_scatter x5 -> x0, waiting for transfers between devices: 350 us -> none  [the longest x1 111 us: shards(): lax.psum_scatter(grad_down_matrix.astype(jnp.bfloat16), 'blk', scatter_di...]
    dot_general x130 -> x20, matrix products: 355 us -> 134 us  [the longest x7 48.5 us: nn(): return jnp.dot(a, b, preferred_element_type=jnp.float32)]
    all_gather x5 -> x0, waiting for transfers between devices: 157 us -> none  [the longest x1 71.5 us: shards(): lax.all_gather(joint_weight, 'blk', axis=0, tiled=True)]
    ppermute x2 -> x6, waiting for transfers between devices: 69.7 us -> 6.95 us  [the longest x1 6.93 us: quick(): lax.ppermute(triple[rows - HALO:, width:], 'blk', [(i, i + 1) for i in ra...]
    psum x2 -> x0, waiting for transfers between devices: 52.6 us -> none  [the longest x1 52.6 us: shards(): lax.psum(share_skip.astype(jnp.bfloat16), 'stream').astype(jnp.float32)]
    unnamed x2 -> x0, blocking collectives: 52.2 us -> none
    dynamic_update_slice x16 -> x0, local copies, waits for them, and re-layouts: 21.5 us -> none  [shards(): mixed, logsum = lax.map(head_forward, (head_query, head_key, head_value))]
  transfers between devices with their start and end apart: 14 -> 6, of which waited for: 10 -> 1; matrix products, arithmetic and copies ran while one was open for 22% -> 19% of each run, Pallas kernels for 0% -> 0%
where the time goes in v1:
time: 695 us; the launch traced here: 684 us
  Pallas kernels  415 us (60%)
  matrix products  134 us (19%)
  local copies, waits for them, and re-layouts  62 us (9%)
  other arithmetic  57.3 us (8%)
  waiting for transfers between devices  6.95 us (1%)
    pallas_call x1, Pallas kernels, reduce_grads(): pl.pallas_call(reduce_kernel, out_shape=[jax.ShapeDtypeStruct((2 * PART,...  215 us
    pallas_call x1, Pallas kernels, gather_weights(): pl.pallas_call(gather_kernel, out_shape=[jax.ShapeDtypeStruct((8, *SMALL)...  131 us
    dot_general x7, matrix products, nn(): return jnp.dot(a, b, preferred_element_type=jnp.float32)  48.5 us
    dot_general x6, matrix products, nt(): lax.dot_general(a, b, (((1,), (1,)), ((), ())), preferred_element_type=jn...  46.4 us
    pallas_call x1, Pallas kernels, attend_back(): pl.pallas_call(attend_back_kernel, out_shape=[jax.ShapeDtypeStruct((rows,...  43.4 us
    dot_general x7, matrix products, tn(): lax.dot_general(a, b, (((0,), (0,)), ((), ())), preferred_element_type=jn...  39.6 us
    convert_element_type x4, other arithmetic, chip(): return (mine.astype(f32) + received.astype(f32)).astype(bf16)  26.1 us
    pallas_call x1, Pallas kernels, attend(): pl.pallas_call(attend_kernel, out_shape=[jax.ShapeDtypeStruct((rows, HEAD...  26 us
  transfers between devices with their start and end apart: 6, of which 1 were waited for; matrix products, arithmetic and copies ran while one was open for 19% of the time, Pallas kernels for 0%

profile of v1, /device:TPU:12, one launch (start us, length us, event | category | flops | bytes accessed | tf_op | source)
XLA Modules:
  0.0 684.2 jit_solution(5773111724472545319)
XLA Ops:
  0.7 6.1 concatenate.31
  6.8 131.0 %shard_map.305 = (bf16[8,16,128]{2,1,0:T(8,128)(2,1)}, bf16[8,288,1152]{2,1,0:T(8,128)(2,1)}, bf16[8,144,4608]{2,1,0:T(8,128)(2,1)}, bf16[8,144,4608]{2,1,0:T(8,128)(2,1)}, bf16[8,576,1152]{2,1,0:T(8,128)(2,1)}) custom-call(bf16[16,128]{1,0:T(8,128)(2,1)} %bitcast.126, bf16[288,1152]{1,0:T(8,128)(2,1)} %refs_1_.1, bf16[144,3456]{1,0:T(8,128)(2,1)} %refs_2_.1, ...), custom_call_target="tpu_custom_call" | custom-call | tf_op jit(solution)/shard_map/pallas_call | solution.py:288
  149.2 8.4 %fusion.16 = bf16[512,3456]{1,0:T(8,128)(2,1)S(1)} fusion(bf16[1152,4608]{1,0:T(8,128)(2,1)} %bitcast.130, f32[1152,512]{1,0:T(8,128)S(1)} %get-tuple-element.138, f32[1152]{0:T(1024)} %reshape.283, f32[1152]{0:T(1024)S(1)} %reshape.282, f32[512]{0:T(512)S(1)} %add_rsqrt_fusion.2, f32[512]{0:T(512)S(1)} %broadcast_multiply_fusion.6), kind=kOutput, calls=%fused_computation.34 | convolution fusion | flops 4081582080 | bytes 13877760 | tf_op jit(solution)/shard_map/dot_general | solution.py:623
  170.6 3.5 fusion.28
  174.2 6.9 %collective-permute-done = bf16[320,2304]{1,0:T(8,128)(2,1)} collective-permute-done((bf16[320,2304]{1,0:T(8,128)(2,1)}, bf16[320,2304]{1,0:T(8,128)(2,1)}, u32[]{:S(2)}, u32[]{:S(2)}) %collective-permute-start) | collective-permute-done | bytes 1474592 | tf_op jit(solution)/shard_map/ppermute | solution.py:799
  181.1 3.2 pad_maximum_fusion.1.pairs
  184.4 26.0 %shard_map.306 = (bf16[512,1152]{1,0:T(8,128)(2,1)S(1)}, f32[16,512,1]{2,1,0:T(8,128)}) custom-call(bf16[512,1152]{1,0:T(8,128)(2,1)S(1)} %slice.99.query, bf16[864,2304]{1,0:T(8,128)(2,1)} %pad_maximum_fusion.1.pairs, s32[512,1]{1,0:T(8,128)S(1)} %copy.58.seg_q, s32[1,864]{1,0:T(1,128)S(1)} %broadcast_in_dim.30.seg_k), custom_call_target="tpu_custom_call" | custom-call | tf_op jit(solution)/shard_map/pallas_call | solution.py:664
  210.4 3.9 fusion.51
  215.2 15.5 %fusion.8 = (bf16[512,4608]{1,0:T(8,128)(2,1)S(1)}, bf16[512,4608]{1,0:T(8,128)(2,1)}) fusion(f32[4608]{0:T(1024)S(1)} %copy-done.58, bf16[1152,4608]{1,0:T(8,128)(2,1)} %bitcast.142, f32[512,1152]{0,1:T(8,128)S(1)} %get-tuple-element.140, f32[1152]{0:T(1024)S(1)} %copy-done.68, f32[1152]{0:T(1024)S(1)} %reshape.286, f32[512]{0:T(512)S(1)} %add_rsqrt_fusion.1, ...), kind=kOutput, calls=%fused_computation.19 | convolution fusion | flops 5467078656 | bytes 22445056 | tf_op jit(solution)/shard_map/dot_general | solution.py:623
  230.7 8.7 %convert_reduce_fusion = (f32[4608]{0:T(1024)}, bf16[512,4608]{1,0:T(8,128)(2,1)}) fusion(bf16[512,4608]{1,0:T(8,128)(2,1)S(1)} %get-tuple-element.41, bf16[4608,1152]{1,0:T(8,128)(2,1)S(1)} %bitcast.141, bf16[512,1152]{1,0:T(8,128)(2,1)S(1)} %copy-done.32), kind=kOutput, calls=%fused_computation.22 | convolution fusion | flops 5447609856 | bytes 21252096 | tf_op jit(solution)/shard_map/dot_general | solution.py:615
  239.4 13.0 %fusion.53 = (f32[1152]{0:T(1024)}, f32[512,1152]{1,0:T(8,128)}) fusion(bf16[512,4608]{1,0:T(8,128)(2,1)} %get-tuple-element.147, bf16[1152,4608]{1,0:T(8,128)(2,1)} %bitcast.143), kind=kOutput, calls=%fused_computation.141 | convolution fusion | flops 5436406784 | bytes 17699328 | tf_op jit(solution)/shard_map/dot_general | solution.py:615
  252.4 8.5 %convolution_convert_fusion.1 = bf16[1152,4608]{1,0:T(8,128)(2,1)} fusion(bf16[512,4608]{1,0:T(8,128)(2,1)S(1)} %copy-done.84, f32[512,1152]{0,1:T(8,128)S(1)} %get-tuple-element.140, f32[1152]{0:T(1024)S(1)} %copy-done.68, f32[1152]{0:T(1024)S(1)} %reshape.286, f32[512]{0:T(512)S(1)} %add_rsqrt_fusion.1, f32[512]{0:T(512)S(1)} %broadcast_multiply_fusion.5), kind=kOutput, calls=%fused_computation.2 | convolution fusion | flops 5444075520 | bytes 17708032 | tf_op jit(solution)/shard_map/dot_general | solution.py:619
  261.0 3.3 copy.62
  264.4 3.3 multiply_reduce_fusion
  269.6 5.5 convolution_convert_fusion.6.grad
  275.1 43.4 %shard_map.307 = (bf16[512,1152]{1,0:T(8,128)(2,1)}, bf16[864,2304]{1,0:T(8,128)(2,1)}) custom-call(bf16[512,1152]{1,0:T(8,128)(2,1)} %copy-done.1, bf16[864,2304]{1,0:T(8,128)(2,1)} %pad_maximum_fusion.1.pairs, bf16[512,1152]{1,0:T(8,128)(2,1)} %copy-done.3, bf16[512,1152]{1,0:T(8,128)(2,1)} %convolution_convert_fusion.6.grad, ...), custom_call_target="tpu_custom_call" | custom-call | tf_op jit(solution)/shard_map/pallas_call | solution.py:725
  328.0 5.4 dynamic-slice_bitcast_fusion.1
  334.0 6.6 convolution_convert_fusion
  346.6 13.5 %fusion.34 = bf16[512,1152]{0,1:T(8,128)(2,1)S(1)} fusion(f32[512,1152]{0,1:T(8,128)S(1)} %copy-done.13, bf16[512,4608]{1,0:T(8,128)(2,1)} %get-tuple-element.39, bf16[4608,1152]{1,0:T(8,128)(2,1)} %bitcast.138, f32[1152]{0:T(1024)S(1)} %copy-done.67), kind=kOutput, calls=%fused_computation.60 | convolution fusion | flops 5437587456 | bytes 18878976 | tf_op jit(solution)/shard_map/dot_general | solution.py:623
  361.8 5.1 convolution_convert_fusion.2
  366.9 5.7 multiply_reduce_fusion.8
  374.5 6.9 %fusion.52 = (f32[1152]{0:T(1024)}, f32[512,1152]{1,0:T(8,128)}) fusion(bf16[1152,4608]{1,0:T(8,128)(2,1)S(1)} %bitcast.137, bf16[512,2304]{1,0:T(8,128)(2,1)S(1)} %add_convert_fusion, bf16[512,1152]{1,0:T(8,128)(2,1)S(1)} %copy-done.79), kind=kOutput, calls=%fused_computation.140 | convolution fusion | flops 4084530176 | bytes 13865472 | tf_op jit(solution)/shard_map/dot_general | solution.py:615
  381.4 3.5 copy.64
  384.9 3.3 multiply_reduce_fusion.1
  398.4 8.1 %fusion.37 = f32[1152,3456]{1,0:T(8,128)} fusion(bf16[512,2304]{1,0:T(8,128)(2,1)S(1)} %copy-done.24, bf16[512,1152]{1,0:T(8,128)(2,1)S(1)} %copy-done.80, f32[1152,512]{1,0:T(8,128)S(1)} %copy-done.9, f32[1152]{0:T(1024)S(1)} %copy-done.44, f32[1152]{0:T(1024)S(1)} %reshape.282, f32[512]{0:T(512)S(1)} %copy-done.60, f32[512]{0:T(512)S(1)} %copy-done.41), kind=kOutput, calls=%fused_computation.78 | convolution fusion | flops 4086890496 | bytes 21836800 | tf_op jit(solution)/shard_map/dot_general | solution.py:619
  406.6 7.7 %fusion = bf16[1152,3456]{1,0:T(8,128)(2,1)S(1)} fusion(f32[1152,3456]{1,0:T(8,128)} %fusion.37, bf16[32,2304]{1,0:T(8,128)(2,1)S(1)} %copy-done.36, f32[32,1152]{1,0:T(8,128)S(1)} %copy-done.29, f32[1152]{0:T(1024)S(1)} %copy-done.44, f32[1152]{0:T(1024)S(1)} %reshape.282, f32[32]{0:T(128)S(1)} %copy-done.76, f32[32]{0:T(128)S(1)} %copy-done.73), kind=kOutput, calls=%fused_computation.3 | convolution fusion | flops 262950912 | bytes 24192256 | tf_op jit(solution)/shard_map/dot_general | solution.py:619
  423.5 6.5 convolution_convert_fusion.5
  431.6 3.9 fusion.23.refs_0_
  435.5 7.8 %fusion.1.refs_3_ = bf16[4,576,1152]{2,1,0:T(8,128)(2,1)} fusion(bf16[4,576,1152]{2,1,0:T(8,128)(2,1)} %collective-permute-done.5, bf16[4,2,576,1152]{3,2,1,0:T(8,128)(2,1)} %bitcast.118, s32[]{:T(128)S(6)} %select_n.31), kind=kLoop, calls=%fused_computation.10 | loop fusion | flops 10616832 | bytes 15925252 | tf_op jit(solution)/shard_map/convert_element_type | solution.py:819
  443.4 8.0 %fusion.2.refs_2_ = bf16[4,144,4608]{2,1,0:T(8,128)(2,1)} fusion(bf16[4,144,4608]{2,1,0:T(8,128)(2,1)} %collective-permute-done.4, bf16[4,2,144,4608]{3,2,1,0:T(8,128)(2,1)} %bitcast.116, s32[]{:T(128)S(6)} %select_n.31), kind=kLoop, calls=%fused_computation.12 | loop fusion | flops 10616832 | bytes 15925252 | tf_op jit(solution)/shard_map/convert_element_type | solution.py:819
  451.4 6.4 fusion.3.refs_1_
  457.8 214.6 %shard_map.308 = (bf16[288,1152]{1,0:T(8,128)(2,1)}, bf16[144,4608]{1,0:T(8,128)(2,1)}, bf16[144,4608]{1,0:T(8,128)(2,1)}, bf16[576,1152]{1,0:T(8,128)(2,1)}, f3...) custom-call(bf16[4,288,1152]{2,1,0:T(8,128)(2,1)} %fusion.23.refs_0_, bf16[4,144,4608]{2,1,0:T(8,128)(2,1)} %fusion.3.refs_1_, ...), custom_call_target="tpu_custom_call" | custom-call | tf_op jit(solution)/shard_map/pallas_call | solution.py:591
  (293 shorter events, 78.3 us)
Async XLA Ops:
  0.7 144.1 %copy-start = (bf16[512,1152]{1,0:T(8,128)(2,1)S(1)}, bf16[512,1152]{1,0:T(8,128)(2,1)}, u32[]{:S(2)}) copy-start(bf16[512,1152]{1,0:T(8,128)(2,1)} %param.19) | copy-start | bytes 3538948
  146.7 10.9 %copy-start.7 = (f32[1152,512]{1,0:T(8,128)}, f32[1152,512]{1,0:T(8,128)S(1)}, u32[]{:S(2)}) copy-start(f32[1152,512]{1,0:T(8,128)S(1)} %get-tuple-element.138) | copy-start | bytes 7077892
  146.7 10.9 %copy-start.40 = (f32[512]{0:T(512)}, f32[512]{0:T(512)S(1)}, u32[]{:S(2)}) copy-start(f32[512]{0:T(512)S(1)} %broadcast_multiply_fusion.6) | copy-start | bytes 6148
  147.0 10.6 %copy-start.59 = (f32[512]{0:T(512)}, f32[512]{0:T(512)S(1)}, u32[]{:S(2)}) copy-start(f32[512]{0:T(512)S(1)} %add_rsqrt_fusion.2) | copy-start | bytes 6148
  159.0 22.2 %collective-permute-start = (bf16[320,2304]{1,0:T(8,128)(2,1)}, bf16[320,2304]{1,0:T(8,128)(2,1)}, u32[]{:S(2)}, u32[]{:S(2)}) collective-permute-start(bf16[320,2304]{1,0:T(8,128)(2,1)} %slice.100), channel_id=1, source_target_pairs={{0,1},{1,2},{2,3},{3,4},{4,5},{5,6},{6,7},{8,9},{9,10},{10,11},{11... | collective-permute-start | bytes 4423688 | tf_op jit(solution)/shard_map/ppermute | solution.py:799
  163.9 20.4 %copy-start.1 = (bf16[512,1152]{1,0:T(8,128)(2,1)}, bf16[512,1152]{1,0:T(8,128)(2,1)S(1)}, u32[]{:S(2)}) copy-start(bf16[512,1152]{1,0:T(8,128)(2,1)S(1)} %slice.99.query) | copy-start | bytes 3538948
  164.0 10.1 %copy-start.74 = (f32[32]{0:T(128)}, f32[32]{0:T(128)S(1)}, u32[]{:S(2)}) copy-start(f32[32]{0:T(128)S(1)} %rsqrt.29) | copy-start | bytes 388
  164.5 19.8 %copy-start.2 = (s32[512,1]{1,0:T(8,128)}, s32[512,1]{1,0:T(8,128)S(1)}, u32[]{:S(2)}) copy-start(s32[512,1]{1,0:T(8,128)S(1)} %copy.58.seg_q) | copy-start | bytes 6148
  164.6 19.7 %copy-start.5 = (s32[1,864]{1,0:T(1,128)}, s32[1,864]{1,0:T(1,128)S(1)}, u32[]{:S(2)}) copy-start(s32[1,864]{1,0:T(1,128)S(1)} %broadcast_in_dim.30.seg_k) | copy-start | bytes 10372
  170.6 10.5 %slice-start.4 = ((bf16[512,3456]{1,0:T(8,128)(2,1)}), bf16[512,2304]{1,0:T(8,128)(2,1)S(1)}, s32[]{:S(2)}) async-start(bf16[512,3456]{1,0:T(8,128)(2,1)} %copy-done.20), calls=%async_computation.4 | async-start | bytes 4718592 | tf_op jit(solution)/shard_map/slice | solution.py:800
  184.3 26.1 %copy-start.8 = (f32[1152,512]{1,0:T(8,128)S(1)}, f32[1152,512]{1,0:T(8,128)}, u32[]{:S(2)}) copy-start(f32[1152,512]{1,0:T(8,128)} %copy-done.7) | copy-start | bytes 7077892
  184.3 26.1 %copy-start.70 = (f32[1152]{0:T(1024)S(1)}, f32[1152]{0:T(1024)}, u32[]{:S(2)}) copy-start(f32[1152]{0:T(1024)} %reshape.285) | copy-start | bytes 13828
  214.4 53.3 %copy-start.12 = (f32[512,1152]{0,1:T(8,128)}, f32[512,1152]{0,1:T(8,128)S(1)}, u32[]{:S(2)}) copy-start(f32[512,1152]{0,1:T(8,128)S(1)} %get-tuple-element.140) | copy-start | bytes 7077892
  214.4 38.0 %copy-start.55 = (f32[512]{0:T(512)}, f32[512]{0:T(512)S(1)}, u32[]{:S(2)}) copy-start(f32[512]{0:T(512)S(1)} %broadcast_multiply_fusion.5) | copy-start | bytes 6148
  214.4 16.2 %slice-start.8 = ((s8[10616832]{0:T(1024)(128)(4,1)}), s8[4194304]{0:T(1024)(128)(4,1)S(1)}, s32[]{:S(2)}) async-start(s8[10616832]{0:T(1024)(128)(4,1)} %bitcast.139), calls=%async_computation.8 | async-start | bytes 8388608
  214.7 37.7 %copy-start.61 = (f32[512]{0:T(512)}, f32[512]{0:T(512)S(1)}, u32[]{:S(2)}) copy-start(f32[512]{0:T(512)S(1)} %add_rsqrt_fusion.1) | copy-start | bytes 6148
  215.2 15.5 %copy-start.32 = (bf16[512,1152]{1,0:T(8,128)(2,1)S(1)}, bf16[512,1152]{1,0:T(8,128)(2,1)}, u32[]{:S(2)}) copy-start(bf16[512,1152]{1,0:T(8,128)(2,1)} %param.35) | copy-start | bytes 3538948
  215.2 15.5 %slice-start.9 = ((s8[10616832]{0:T(1024)(128)(4,1)}), s8[4194304]{0:T(1024)(128)(4,1)S(1)}, s32[]{:S(2)}) async-start(s8[10616832]{0:T(1024)(128)(4,1)} %bitcast.139), calls=%async_computation.9 | async-start | bytes 8388608
  215.2 15.5 %slice-start.10 = ((s8[10616832]{0:T(1024)(128)(4,1)}), s8[2228224]{0:T(1024)(128)(4,1)S(1)}, s32[]{:S(2)}) async-start(s8[10616832]{0:T(1024)(128)(4,1)} %bitcast.139), calls=%async_computation.10 | async-start | bytes 4456448
  239.4 13.0 %copy-start.84 = (bf16[512,4608]{1,0:T(8,128)(2,1)S(1)}, bf16[512,4608]{1,0:T(8,128)(2,1)}, u32[]{:S(2)}) copy-start(bf16[512,4608]{1,0:T(8,128)(2,1)} %get-tuple-element.147) | copy-start | bytes 14155780
  318.5 15.5 %slice-start.11 = ((s8[4718592]{0:T(1024)(128)(4,1)}), s8[524288]{0:T(1024)(128)(4,1)S(1)}, s32[]{:S(2)}) async-start(s8[4718592]{0:T(1024)(128)(4,1)} %bitcast.144), calls=%async_computation.11 | async-start | bytes 1048576
  322.7 49.9 %collective-permute-start.1 = (bf16[320,2304]{1,0:T(8,128)(2,1)}, bf16[320,2304]{1,0:T(8,128)(2,1)}, u32[]{:S(2)}, u32[]{:S(2)}) collective-permute-start(bf16[320,2304]{1,0:T(8,128)(2,1)} %slice.91), channel_id=1, source_target_pairs={{1,0},{2,1},{3,2},{4,3},{5,4},{6,5},{7,6},{9,8},{10,9},{11,10},{12... | collective-permute-start | bytes 4423688 | tf_op jit(solution)/shard_map/ppermute | solution.py:835
  333.5 109.9 %collective-permute-start.4 = (bf16[4,144,4608]{2,1,0:T(8,128)(2,1)}, bf16[4,144,4608]{2,1,0:T(8,128)(2,1)}, u32[]{:S(2)}, u32[]{:S(2)}) collective-permute-start(bf16[4,144,4608]{2,1,0:T(8,128)(2,1)} %dynamic-slice_bitcast_fusion.1), channel_id=1, source_target_pairs={{0,1},{1,0},{2,3},{3,2},{4,5},{5,4},{6,7},{7,6},{8,9},{9,8},{10,11... | collective-permute-start | bytes 15925256 | tf_op jit(solution)/shard_map/ppermute | solution.py:818
  346.6 15.1 %copy-start.4 = (bf16[512,1152]{1,0:T(8,128)(2,1)S(1)}, bf16[512,1152]{1,0:T(8,128)(2,1)}, u32[]{:S(2)}) copy-start(bf16[512,1152]{1,0:T(8,128)(2,1)} %copy-done.3) | copy-start | bytes 3538948
  346.6 88.9 %collective-permute-start.5 = (bf16[4,576,1152]{2,1,0:T(8,128)(2,1)}, bf16[4,576,1152]{2,1,0:T(8,128)(2,1)}, u32[]{:S(2)}, u32[]{:S(2)}) collective-permute-start(bf16[4,576,1152]{2,1,0:T(8,128)(2,1)} %dynamic-slice_bitcast_fusion), channel_id=1, source_target_pairs={{0,1},{1,0},{2,3},{3,2},{4,5},{5,4},{6,7},{7,6},{8,9},{9,8},{10,11... | collective-permute-start | bytes 15925256 | tf_op jit(solution)/shard_map/ppermute | solution.py:818
  361.8 12.7 %slice-start.5 = ((s8[10616832]{0:T(1024)(128)(4,1)}), s8[4194304]{0:T(1024)(128)(4,1)S(1)}, s32[]{:S(2)}) async-start(s8[10616832]{0:T(1024)(128)(4,1)} %bitcast.135), calls=%async_computation.5 | async-start | bytes 8388608
  361.8 12.7 %slice-start.6 = ((s8[10616832]{0:T(1024)(128)(4,1)}), s8[4194304]{0:T(1024)(128)(4,1)S(1)}, s32[]{:S(2)}) async-start(s8[10616832]{0:T(1024)(128)(4,1)} %bitcast.135), calls=%async_computation.6 | async-start | bytes 8388608
  397.7 33.9 %collective-permute-start.2 = (bf16[4,288,1152]{2,1,0:T(8,128)(2,1)}, bf16[4,288,1152]{2,1,0:T(8,128)(2,1)}, u32[]{:S(2)}, u32[]{:S(2)}) collective-permute-start(bf16[4,288,1152]{2,1,0:T(8,128)(2,1)} %dynamic-slice_bitcast_fusion.2), channel_id=1, source_target_pairs={{0,1},{1,0},{2,3},{3,2},{4,5},{5,4},{6,7},{7,6},{8,9},{9,8},{10,11... | collective-permute-start | bytes 7962632 | tf_op jit(solution)/shard_map/ppermute | solution.py:818
  414.5 9.0 %copy-start.31 = (bf16[512,1152]{0,1:T(8,128)(2,1)S(1)}, bf16[512,1152]{0,1:T(8,128)(2,1)}, u32[]{:S(2)}) copy-start(bf16[512,1152]{0,1:T(8,128)(2,1)} %copy-done.30) | copy-start | bytes 3538948
  419.3 32.1 %collective-permute-start.3 = (bf16[4,144,4608]{2,1,0:T(8,128)(2,1)}, bf16[4,144,4608]{2,1,0:T(8,128)(2,1)}, u32[]{:S(2)}, u32[]{:S(2)}) collective-permute-start(bf16[4,144,4608]{2,1,0:T(8,128)(2,1)} %fusion.20), channel_id=1, source_target_pairs={{0,1},{1,0},{2,3},{3,2},{4,5},{5,4},{6,7},{7,6},{8,9},{9,8},{10,11... | collective-permute-start | bytes 15925256 | tf_op jit(solution)/shard_map/ppermute | solution.py:818
  419.7 11.9 %slice-start.2 = ((s8[5308416]{0:T(1024)(128)(4,1)}), s8[1114112]{0:T(1024)(128)(4,1)S(1)}, s32[]{:S(2)}) async-start(s8[5308416]{0:T(1024)(128)(4,1)} %bitcast.110), calls=%async_computation.2 | async-start | bytes 2228224
  435.5 15.8 %slice-start = ((s8[7962624]{0:T(1024)(128)(4,1)}), s8[4194304]{0:T(1024)(128)(4,1)S(1)}, s32[]{:S(2)}) async-start(s8[7962624]{0:T(1024)(128)(4,1)} %bitcast.106), calls=%async_computation | async-start | bytes 8388608
  (72 other events, 376.0 us)

commit v2 on v0

--- a/solution.py
+++ b/solution.py
@@ -1,13 +1,1286 @@
+import functools
 from functools import partial
 
 import jax
 import jax.numpy as jnp
 from jax import lax
+from jax.experimental import pallas as pl
+from jax.experimental.pallas import tpu as pltpu
 from jax.sharding import PartitionSpec as P
 
 HEADS = 16
 HEAD = 72
 LEN_MIN = 192
+
+MESH = pl.DeviceIdType.MESH
+ANY = pl.BlockSpec(memory_space=pl.ANY)
+WIDTH = 1152
+PART = 144
+SMALL = (16, 128)
+
+
+class Place:
+    def __init__(self):
+        self.s = lax.axis_index("stream")
+        self.b = lax.axis_index("blk")
+        self.x = lax.rem(self.s, 2)
+        self.y = lax.div(self.s, 2)
+        self.c = lax.rem(self.b, 2)
+        self.zz = lax.div(self.b, 2)
+
+    def flip(self, bit):
+        return 1 - bit
+
+    def other(self, k):
+        low, high = lax.rem(self.zz, 2), lax.div(self.zz, 2)
+        return 2 * (1 - high if k & 2 else high) + (1 - low if k & 1 else low)
+
+    def source(self, k):
+        zz = self.zz
+        table = ((1, 0, 3, 2), (2, 2, 1, 1), (3, 3, 0, 0))[k - 1]
+        return jnp.where(zz < 2, jnp.where(zz == 0, table[0], table[1]), jnp.where(zz == 2, table[2], table[3]))
+
+    def at(self, x=None, y=None, zz=None, c=None):
+        x = self.x if x is None else x
+        y = self.y if y is None else y
+        zz = self.zz if zz is None else zz
+        c = self.c if c is None else c
+        return (2 * y + x, 2 * zz + c)
+
+
+def greet(place):
+    barrier = pltpu.get_barrier_semaphore()
+    near = [
+        place.at(x=1 - place.x),
+        place.at(y=1 - place.y),
+        place.at(c=1 - place.c),
+    ] + [place.at(zz=place.other(k)) for k in (1, 2, 3)]
+    for device in near:
+        pl.semaphore_signal(barrier, inc=1, device_id=device, device_id_type=MESH)
+    pl.semaphore_wait(barrier, len(near))
+
+
+def remote(src, dst, send, recv, device):
+    return pltpu.make_async_remote_copy(
+        src_ref=src, dst_ref=dst, send_sem=send, recv_sem=recv, device_id=device, device_id_type=MESH
+    )
+
+
+def piece(kind, ref, b, x, y):
+    if kind == "cols":
+        return ref.at[b, :, pl.ds(pl.multiple_of((2 * y + x) * WIDTH, 128), WIDTH)]
+    if kind == "rows":
+        return ref.at[b, pl.ds(pl.multiple_of((2 * y + x) * PART, 16), PART)]
+    low, size = (0, 80) if y == 0 else (80, 64)
+    return ref.at[b, pl.ds(pl.multiple_of(x * PART + low, 16), size)]
+
+
+KINDS = ("half", "cols", "cols", "rows")
+
+
+class Gather:
+    SEMS = [pltpu.SemaphoreType.DMA((4, 6, 4, 2)), pltpu.SemaphoreType.DMA((12,)), pltpu.SemaphoreType.DMA((2, 8))]
+
+    def __init__(self, place, shards, outs, scratch):
+        self.place = place
+        self.small_in, self.skip_in, self.joint_in, self.out_in, self.up_in, self.down_in = shards
+        self.small = outs[0]
+        self.outs = outs[1:]
+        self.sems, self.local_sems, self.small_sems = scratch[:3]
+        self.stage = scratch[3:]
+        self.sent = []
+
+    def copy(self, t, x, y, zz, c, stage, k, device):
+        ref = piece(KINDS[t], self.outs[t], 2 * zz + c, x, y)
+        return remote(ref, ref, self.sems.at[t, stage, k, 0], self.sems.at[t, stage, k, 1], device)
+
+    def each_y(self, t, run):
+        if KINDS[t] != "half":
+            run(self.place.y)
+            return
+        for value in (0, 1):
+            pl.when(self.place.y == value)(lambda value=value: run(value))
+
+    STAGE = [
+        pltpu.VMEM((2 * PART, WIDTH), jnp.bfloat16),
+        pltpu.VMEM((PART, 4 * WIDTH), jnp.bfloat16),
+        pltpu.VMEM((PART, 4 * WIDTH), jnp.bfloat16),
+        pltpu.VMEM((4 * PART, WIDTH), jnp.bfloat16),
+    ]
+
+    def locals(self, t):
+        if t == 1:
+            return [
+                (self.joint_in, self.stage[1].at[:, pl.ds(0, 3 * WIDTH)]),
+                (self.out_in, self.stage[1].at[:, pl.ds(3 * WIDTH, WIDTH)]),
+            ]
+        return [({0: self.skip_in, 2: self.up_in, 3: self.down_in}[t], self.stage[t])]
+
+    def own_start(self, t):
+        for i, (src, dst) in enumerate(self.locals(t)):
+            pltpu.make_async_copy(src, dst, self.local_sems.at[2 * t + i]).start()
+
+    def own_keep(self, t):
+        return pltpu.make_async_copy(self.stage[t], self.outs[t].at[self.place.b], self.local_sems.at[8 + t])
+
+    def own_done(self, t):
+        for i, (src, dst) in enumerate(self.locals(t)):
+            pltpu.make_async_copy(src, dst, self.local_sems.at[2 * t + i]).wait()
+        self.own_keep(t).start()
+
+    def own_copy(self, t, c):
+        ref = self.outs[t].at[2 * self.place.zz + c]
+        src = self.stage[t]
+        sems = self.sems.at[t, 4, 0]
+        return remote(src, ref, sems.at[0], sems.at[1], self.place.at(c=1 - self.place.c))
+
+    def small_start(self):
+        p = self.place
+        for i, device in enumerate([p.at(zz=p.other(k)) for k in (1, 2, 3)] + [p.at(c=1 - p.c)]):
+            remote(self.small_in, self.small.at[p.b], self.small_sems.at[0, i], self.small_sems.at[1, i], device).start()
+        pltpu.make_async_copy(self.small_in, self.small.at[p.b], self.small_sems.at[0, 7]).start()
+
+    def small_pass(self):
+        p = self.place
+        for i, k in enumerate((1, 2, 3)):
+            ref = self.small.at[2 * p.other(k) + p.c]
+            remote(ref, ref, self.small_sems.at[0, i], self.small_sems.at[1, i], p.at()).wait_recv()
+            remote(ref, ref, self.small_sems.at[0, 4 + i], self.small_sems.at[1, 4 + i], p.at(c=1 - p.c)).start()
+
+    def small_done(self):
+        p = self.place
+        for i, k in enumerate((0, 1, 2, 3)):
+            ref = self.small.at[2 * p.other(k) + 1 - p.c]
+            remote(ref, ref, self.small_sems.at[0, 3 + i], self.small_sems.at[1, 3 + i], p.at()).wait_recv()
+        for i in range(7):
+            remote(self.small_in, self.small_in, self.small_sems.at[0, i], self.small_sems.at[1, i], p.at()).wait_send()
+        pltpu.make_async_copy(self.small_in, self.small.at[p.b], self.small_sems.at[0, 7]).wait()
+
+    def stage_piece(self, t, y):
+        x = self.place.x
+        q = 2 * y + x
+        if KINDS[t] == "cols":
+            return self.stage[t].at[:, pl.ds(pl.multiple_of(q * WIDTH, 128), WIDTH)]
+        if KINDS[t] == "rows":
+            return self.stage[t].at[pl.ds(pl.multiple_of(q * PART, 16), PART)]
+        low, size = (0, 80) if y == 0 else (80, 64)
+        return self.stage[t].at[pl.ds(pl.multiple_of(x * PART + low, 16), size)]
+
+    def z_copies(self, t, y, zz, start, own=False):
+        p = self.place
+        for step, send in ((1, 0), (-1, 5)):
+            go = (zz <= p.zz) & (p.zz < 3) if step == 1 else (zz >= p.zz) & (p.zz > 0)
+            ref = piece(KINDS[t], self.outs[t], 2 * zz + p.c, p.x, y)
+
+            @pl.when(go)
+            def _():
+                copy = remote(self.stage_piece(t, y) if own else ref, ref, self.sems.at[t, send, zz, 0], self.sems.at[t, 0, zz, 1], p.at(zz=p.zz + step))
+                copy.start() if start else copy.wait_send()
+
+    def z_start(self, t):
+        p = self.place
+        self.each_y(t, lambda y: self.z_copies(t, y, p.zz, True, True))
+        self.own_copy(t, p.c).start()
+
+    def z_done(self, t, k):
+        p = self.place
+        zz = p.source(k)
+
+        def run(y):
+            self.copy(t, p.x, y, zz, p.c, 0, zz, p.at()).wait_recv()
+            self.copy(t, p.x, y, zz, p.c, 1, k, p.at(x=1 - p.x)).start()
+            self.copy(t, p.x, y, zz, p.c, 2, k, p.at(y=1 - p.y)).start()
+            self.z_copies(t, y, zz, True)
+
+        self.each_y(t, run)
+
+    def by_x(self, t, k):
+        return k == 1 or (k == 2 and t % 2 == 0)
+
+    def xy_done(self, t, k):
+        p = self.place
+
+        def run(y):
+            zz = p.source(k)
+            self.copy(t, 1 - p.x, y, zz, p.c, 1, k, p.at()).wait_recv()
+            if self.by_x(t, k):
+                self.copy(t, 1 - p.x, y, zz, p.c, 3, k, p.at(y=1 - p.y)).start()
+            self.copy(t, p.x, 1 - y, zz, p.c, 2, k, p.at()).wait_recv()
+            if not self.by_x(t, k):
+                self.copy(t, p.x, 1 - y, zz, p.c, 3, k, p.at(x=1 - p.x)).start()
+
+        self.each_y(t, run)
+
+    def diag_done(self, t, k):
+        p = self.place
+
+        def run(y):
+            zz = p.source(k)
+            self.copy(t, 1 - p.x, 1 - y, zz, p.c, 3, k, p.at()).wait_recv()
+
+        self.each_y(t, run)
+        self.pair_copy(t, k, p.c).start()
+
+    def pair_copy(self, t, k, c):
+        ref = self.outs[t].at[2 * self.place.source(k) + c]
+        sems = self.sems.at[t, 4, k]
+        return remote(ref, ref, sems.at[0], sems.at[1], self.place.at(c=1 - self.place.c))
+
+    def ready(self, t):
+        p = self.place
+        self.own_copy(t, 1 - p.c).wait_recv()
+        for k in (1, 2, 3):
+            self.pair_copy(t, k, 1 - p.c).wait_recv()
+
+    def all_sent(self, t):
+        p = self.place
+        self.own_copy(t, p.c).wait_send()
+        self.own_keep(t).wait()
+
+        def run(y):
+            self.z_copies(t, y, p.zz, False, True)
+            for k in (1, 2, 3):
+                zz = p.source(k)
+                self.z_copies(t, y, zz, False)
+                self.copy(t, p.x, y, zz, p.c, 1, k, p.at()).wait_send()
+                self.copy(t, p.x, y, zz, p.c, 2, k, p.at()).wait_send()
+                if self.by_x(t, k):
+                    self.copy(t, 1 - p.x, y, zz, p.c, 3, k, p.at()).wait_send()
+                else:
+                    self.copy(t, p.x, 1 - y, zz, p.c, 3, k, p.at()).wait_send()
+
+        self.each_y(t, run)
+        for k in (1, 2, 3):
+            self.pair_copy(t, k, p.c).wait_send()
+
+
+def gather_kernel(*refs):
+    shards, outs, scratch = refs[:6], refs[6:11], refs[11:]
+    place = Place()
+    g = Gather(place, shards, outs, scratch)
+    for t in range(4):
+        g.own_start(t)
+    greet(place)
+    g.small_start()
+    g.own_done(0)
+    g.z_start(0)
+    g.small_pass()
+    for t in range(4):
+        for k in (1, 2, 3):
+            g.z_done(t, k)
+        if t + 1 < 4:
+            g.own_done(t + 1)
+            g.z_start(t + 1)
+        if t > 0:
+            for k in (1, 2, 3):
+                g.diag_done(t - 1, k)
+        for k in (1, 2, 3):
+            g.xy_done(t, k)
+    for k in (1, 2, 3):
+        g.diag_done(3, k)
+    g.small_done()
+    for t in range(4):
+        g.ready(t)
+        g.all_sent(t)
+
+
+def gather_weights(small, skip, joint, out, up, down):
+    bf16 = jnp.bfloat16
+    return pl.pallas_call(
+        gather_kernel,
+        out_shape=[
+            jax.ShapeDtypeStruct((8, *SMALL), bf16),
+            jax.ShapeDtypeStruct((8, 2 * PART, WIDTH), bf16),
+            jax.ShapeDtypeStruct((8, PART, 4 * WIDTH), bf16),
+            jax.ShapeDtypeStruct((8, PART, 4 * WIDTH), bf16),
+            jax.ShapeDtypeStruct((8, 4 * PART, WIDTH), bf16),
+        ],
+        in_specs=[ANY] * 6,
+        out_specs=[ANY] * 5,
+        scratch_shapes=Gather.SEMS + Gather.STAGE,
+        compiler_params=pltpu.CompilerParams(collective_id=0, has_side_effects=True),
+    )(small, skip, joint, out, up, down)
+
+
+SIZES = (80, PART, PART, PART)
+
+
+HALO = 320
+COND = 32
+TILES = ((0, 0), (256, 256))
+LOG2E = 1.4426950408889634
+
+
+def nt(a, b):
+    return lax.dot_general(a, b, (((1,), (1,)), ((), ())), preferred_element_type=jnp.float32)
+
+
+def tn(a, b):
+    return lax.dot_general(a, b, (((0,), (0,)), ((), ())), preferred_element_type=jnp.float32)
+
+
+def nn(a, b):
+    return jnp.dot(a, b, preferred_element_type=jnp.float32)
+
+
+def make_bias(seg_q, seg_k, bias):
+    bias[...] = jnp.where(seg_q[...] == seg_k[...], 0.0, -1e30)
+
+
+def head(h):
+    return slice(HEAD * h, HEAD * (h + 1))
+
+
+def attend_kernel(query, pairs, seg_q, seg_k, attended, logsum, heads_q, heads_k, heads_v, heads_o, bias):
+    make_bias(seg_q, seg_k, bias)
+    for h in range(HEADS):
+        heads_q[h] = query[:, head(h)]
+        heads_k[h] = pairs[:, head(h)]
+        heads_v[h] = pairs[:, HEADS * HEAD + HEAD * h : HEADS * HEAD + HEAD * (h + 1)]
+
+    @pl.loop(0, HEADS)
+    def _(h):
+        for row, low in TILES:
+            rows, keys = pl.ds(row, 256), pl.ds(low, HALO + 512 + COND - low)
+            scores = nt(heads_q[h, rows], heads_k[h, keys]) * (HEAD**-0.5 * LOG2E) + bias[rows, keys]
+            top = jnp.max(scores, axis=1, keepdims=True)
+            expo = jnp.exp2(scores - top)
+            total = jnp.sum(expo, axis=1, keepdims=True)
+            mixed = nn(expo.astype(jnp.bfloat16), heads_v[h, keys])
+            heads_o[h, rows] = (mixed / total).astype(jnp.bfloat16)
+            logsum[h, rows] = top + jnp.log2(total)
+
+    for h in range(HEADS):
+        attended[:, head(h)] = heads_o[h]
+
+
+def vmem(shape, dtype):
+    return pltpu.VMEM(shape, dtype)
+
+
+def attend(query, pairs, seg_q, seg_k):
+    rows, keys = query.shape[0], pairs.shape[0]
+    bf16 = jnp.bfloat16
+    return pl.pallas_call(
+        attend_kernel,
+        out_shape=[
+            jax.ShapeDtypeStruct((rows, HEADS * HEAD), bf16),
+            jax.ShapeDtypeStruct((HEADS, rows, 1), jnp.float32),
+            jax.ShapeDtypeStruct((HEADS, rows, HEAD), bf16),
+            jax.ShapeDtypeStruct((HEADS, keys, HEAD), bf16),
+            jax.ShapeDtypeStruct((HEADS, keys, HEAD), bf16),
+            jax.ShapeDtypeStruct((HEADS, rows, HEAD), bf16),
+        ],
+        scratch_shapes=[vmem((rows, keys), jnp.float32)],
+        compiler_params=pltpu.CompilerParams(vmem_limit_bytes=50 << 20),
+    )(query, pairs, seg_q, seg_k)
+
+
+TOK = 512
+ROWS8 = 16
+ORDER = (0, 2, 1, 3)
+LITTLE = (16, 256)
+UNIT = (PART, WIDTH)
+
+
+def add_into(out, *ins):
+    @pl.loop(0, out.shape[0] // 16)
+    def _(i):
+        rows = pl.ds(pl.multiple_of(i * 16, 16), 16)
+        total = ins[0][rows].astype(jnp.float32)
+        for ref in ins[1:]:
+            total += ref[rows].astype(jnp.float32)
+        out[rows] = total.astype(out.dtype)
+
+
+class Sum:
+    SEMS = [
+        pltpu.SemaphoreType.DMA((4, 4, 2, 2)),
+        pltpu.SemaphoreType.DMA((4, 4, 2)),
+        pltpu.SemaphoreType.DMA((4, 4, 2)),
+        pltpu.SemaphoreType.DMA((4, 4, 2)),
+        pltpu.SemaphoreType.DMA((23,)),
+    ]
+    SLOTS = [pltpu.VMEM((23, *UNIT), jnp.bfloat16), pltpu.VMEM((4, *UNIT), jnp.bfloat16)]
+    LANDS = [
+        jax.ShapeDtypeStruct(lead + (size, WIDTH), jnp.bfloat16)
+        for size in SIZES
+        for lead in ((4, 2), (4,), (4,))
+    ]
+    PARTS = [
+        jax.ShapeDtypeStruct((8, PART, WIDTH), jnp.bfloat16),
+        jax.ShapeDtypeStruct((4, PART, 4 * WIDTH), jnp.bfloat16),
+        jax.ShapeDtypeStruct((4, PART, 4 * WIDTH), jnp.bfloat16),
+        jax.ShapeDtypeStruct((4, 4, PART, WIDTH), jnp.bfloat16),
+    ]
+
+    def __init__(self, place, parts, lands, outs, sems, slots):
+        self.place, self.parts, self.outs = place, parts, outs
+        self.sem1, self.sem2, self.sem3, self.sem4, self.load_sems = sems
+        self.slots, self.fins = slots
+        self.land1, self.land2, self.land3 = ([lands[3 * t + i] for t in range(4)] for i in range(3))
+
+    def slot(self, t, i):
+        return self.slots.at[i, pl.ds(0, SIZES[t])]
+
+    def fin(self, t):
+        return self.fins.at[t, pl.ds(0, SIZES[t])]
+
+    def piece(self, t, zz, x, y):
+        ref = self.parts[t]
+        if t == 0:
+            return ref.at[2 * zz + x, pl.ds(pl.multiple_of(64 * y, 16), 80)]
+        if t == 3:
+            return ref.at[zz, 2 * y + x]
+        return ref.at[zz, :, pl.ds(pl.multiple_of((2 * y + x) * WIDTH, 128), WIDTH)]
+
+    def half(self, t, zz, x, y, j):
+        return self.piece(t, zz, x, j) if zz < 2 else self.piece(t, zz, j, y)
+
+    def keep(self, zz):
+        return self.place.y if zz < 2 else self.place.x
+
+    def first(self, t, zz, j):
+        p = self.place
+        device = p.at(x=1 - p.x) if zz < 2 else p.at(y=1 - p.y)
+        sems = self.sem1.at[t, zz, j]
+        src = self.half(t, zz, 1 - p.x, 1 - p.y, j)
+        return remote(src, self.land1[t].at[zz, j], sems.at[0], sems.at[1], device)
+
+    def start(self, t, zzs=ORDER):
+        for zz in zzs:
+            for j in (0, 1):
+                self.first(t, zz, j).start()
+
+    def load(self, t, src, i):
+        return pltpu.make_async_copy(src, self.slot(t, i), self.load_sems.at[i])
+
+    def second(self, t, zz):
+        p = self.place
+        device = p.at(y=1 - p.y) if zz < 2 else p.at(x=1 - p.x)
+        sems = self.sem2.at[t, zz]
+        return remote(self.slot(t, 2 * zz), self.land2[t].at[zz], sems.at[0], sems.at[1], device)
+
+    def pass_on(self, t, after=None):
+        p = self.place
+        if after is not None:
+            for zz in ORDER:
+                self.second(after, zz).wait_send()
+
+        def own(zz):
+            return self.load(t, self.half(t, zz, p.x, p.y, 1 - self.keep(zz)), 2 * zz)
+
+        def landed(zz):
+            return self.load(t, self.land1[t].at[zz, 1 - self.keep(zz)], 2 * zz + 1)
+
+        for zz in ORDER:
+            own(zz).start()
+        for zz in ORDER:
+            for j in (0, 1):
+                self.first(t, zz, j).wait_recv()
+            landed(zz).start()
+        for zz in ORDER:
+            own(zz).wait()
+            landed(zz).wait()
+            add_into(self.slot(t, 2 * zz), self.slot(t, 2 * zz), self.slot(t, 2 * zz + 1))
+            self.second(t, zz).start()
+
+    def third(self, t, zz, slot):
+        p = self.place
+        return remote(
+            self.slot(t, 8 + 3 * zz), self.land3[t].at[slot], self.sem3.at[t, zz, 0], self.sem3.at[t, slot, 1],
+            p.at(zz=zz),
+        )
+
+    def third_sent(self, t):
+        for zz in range(4):
+            pl.when(zz != self.place.zz)(lambda zz=zz: self.third(t, zz, self.place.zz).wait_send())
+
+    def to_chip(self, t, after=None):
+        p = self.place
+        if after is not None:
+            self.third_sent(after)
+
+        def load(zz, n):
+            keep = self.keep(zz)
+            if n == 0:
+                src = self.half(t, zz, p.x, p.y, keep)
+            else:
+                src = self.land1[t].at[zz, keep] if n == 1 else self.land2[t].at[zz]
+            return self.load(t, src, 8 + 3 * zz + n)
+
+        for zz in ORDER:
+            load(zz, 0).start()
+            load(zz, 1).start()
+        for zz in ORDER:
+            self.second(t, zz).wait_recv()
+            load(zz, 2).start()
+        for zz in ORDER:
+            for n in range(3):
+                load(zz, n).wait()
+            base = 8 + 3 * zz
+            mine = self.slot(t, base)
+            add_into(mine, mine, self.slot(t, base + 1), self.slot(t, base + 2))
+
+            @pl.when(zz != p.zz)
+            def _():
+                self.third(t, zz, p.zz).start()
+
+            @pl.when(zz == p.zz)
+            def _():
+                add_into(self.fin(t), mine)
+
+    def result(self, t, x, y):
+        ref = self.outs[t]
+        if KINDS[t] == "cols":
+            return ref.at[:, pl.ds(pl.multiple_of((2 * y + x) * WIDTH, 128), WIDTH)]
+        if KINDS[t] == "rows":
+            return ref.at[pl.ds(pl.multiple_of((2 * y + x) * PART, 16), PART)]
+        low, size = (0, 80) if y == 0 else (80, 64)
+        return ref.at[pl.ds(pl.multiple_of(x * PART + low, 16), size)]
+
+    def fin_part(self, t, y):
+        if KINDS[t] != "half" or y == 0:
+            return self.fin(t)
+        return self.fins.at[t, pl.ds(16, 64)]
+
+    def each_y(self, t, run):
+        if KINDS[t] != "half":
+            run(self.place.y)
+            return
+        for value in (0, 1):
+            pl.when(self.place.y == value)(lambda value=value: run(value))
+
+    def spread(self, t, start):
+        p = self.place
+
+        def run(y):
+            src, dst = self.fin_part(t, y), self.result(t, p.x, y)
+            for k in (1, 2, 3):
+                device = p.at(x=1 - p.x if k & 1 else p.x, y=1 - p.y if k & 2 else p.y)
+                sems = self.sem4.at[t, k]
+                copy = remote(src, dst, sems.at[0], sems.at[1], device)
+                copy.start() if start else copy.wait_send()
+            keep = pltpu.make_async_copy(src, dst, self.sem4.at[t, 0, 0])
+            keep.start() if start else keep.wait()
+
+        self.each_y(t, run)
+
+    def finish(self, t):
+        p = self.place
+        for k in (1, 2, 3):
+            ref = self.land3[t].at[p.other(k)]
+            remote(ref, ref, self.sem3.at[t, p.zz, 0], self.sem3.at[t, p.other(k), 1], p.at()).wait_recv()
+            self.load(t, ref, 19 + k).start()
+        for k in (1, 2, 3):
+            self.load(t, self.land3[t].at[p.other(k)], 19 + k).wait()
+        add_into(self.fin(t), self.fin(t), *[self.slot(t, 19 + k) for k in (1, 2, 3)])
+        self.spread(t, True)
+
+    def done(self, t, last):
+        p = self.place
+        for zz in range(4):
+            for j in (0, 1):
+                self.first(t, zz, j).wait_send()
+            if last:
+                self.second(t, zz).wait_send()
+        if last:
+            self.third_sent(t)
+        self.spread(t, False)
+
+        def run(y):
+            for k in (1, 2, 3):
+                ref = self.result(t, 1 - p.x if k & 1 else p.x, 1 - y if k & 2 else y)
+                sems = self.sem4.at[t, k]
+                remote(ref, ref, sems.at[0], sems.at[1], p.at()).wait_recv()
+
+        self.each_y(t, run)
+
+
+class Vectors:
+    SCRATCH = [
+        pltpu.VMEM((8, *LITTLE), jnp.float32),
+        pltpu.VMEM((4, *LITTLE), jnp.float32),
+        pltpu.VMEM((4, *LITTLE), jnp.float32),
+        pltpu.VMEM((4, *LITTLE), jnp.float32),
+        pltpu.VMEM((4, *LITTLE), jnp.float32),
+        pltpu.VMEM((4, *LITTLE), jnp.float32),
+        pltpu.VMEM((COND, WIDTH), jnp.float32),
+        pltpu.VMEM((COND, WIDTH), jnp.float32),
+        pltpu.VMEM((COND, WIDTH), jnp.float32),
+        pltpu.VMEM((4, COND, WIDTH), jnp.float32),
+        pltpu.SemaphoreType.DMA((16, 2)),
+    ]
+
+    def __init__(self, place, small_out, cond_out, scratch):
+        self.place, self.small_out, self.cond_out = place, small_out, cond_out
+        self.part, self.pair, self.x_in, self.sum1, self.y_in, self.z_in = scratch[:6]
+        self.mine, self.cond_pair, self.cond_sum, self.cond_in = scratch[6:10]
+        self.sems = scratch[10]
+
+    def copy(self, i, src, dst, device):
+        return remote(src, dst, self.sems.at[i, 0], self.sems.at[i, 1], device)
+
+    def small_pair(self, zz):
+        p = self.place
+        return self.copy(zz, self.part.at[2 * zz + 1 - p.c], self.pair.at[zz], p.at(c=1 - p.c))
+
+    def run_pair(self):
+        p = self.place
+        for zz in range(4):
+            self.small_pair(zz).start()
+        cond = self.copy(4, self.mine, self.cond_pair, p.at(c=1 - p.c))
+        cond.start()
+        for zz in range(4):
+            self.small_pair(zz).wait()
+            self.pair[zz] += self.part[2 * zz + p.c]
+        cond.wait()
+        self.cond_sum[...] = self.mine[...] + self.cond_pair[...]
+        self.copy(5, self.pair, self.x_in, p.at(x=1 - p.x)).start()
+        for k in (1, 2, 3):
+            self.copy(6 + k, self.cond_sum, self.cond_in.at[p.zz], p.at(zz=p.other(k))).start()
+        self.cond_in[p.zz] = self.cond_sum[...]
+
+    def run_x(self):
+        p = self.place
+        self.copy(5, self.pair, self.x_in, p.at(x=1 - p.x)).wait()
+        self.sum1[...] = self.pair[...] + self.x_in[...]
+        self.copy(6, self.sum1, self.y_in, p.at(y=1 - p.y)).start()
+
+    def run_y(self):
+        p = self.place
+        self.copy(6, self.sum1, self.y_in, p.at(y=1 - p.y)).wait()
+        self.sum1[...] += self.y_in[...]
+        for k in (1, 2, 3):
+            self.copy(9 + k, self.sum1.at[p.other(k)], self.z_in.at[p.zz], p.at(zz=p.other(k))).start()
+        self.z_in[p.zz] = self.sum1[p.zz]
+
+    def run_z(self):
+        p = self.place
+        for k in (1, 2, 3):
+            self.copy(9 + k, self.sum1.at[p.other(k)], self.z_in.at[p.zz], p.at(zz=p.other(k))).wait()
+            self.copy(6 + k, self.cond_sum, self.cond_in.at[p.zz], p.at(zz=p.other(k))).wait()
+        self.small_out[...] = (self.z_in[0] + self.z_in[1]) + (self.z_in[2] + self.z_in[3])
+        cond = (self.cond_in[0] + self.cond_in[1]) + (self.cond_in[2] + self.cond_in[3])
+        self.cond_out[...] = cond.astype(jnp.bfloat16)
+
+
+class Names:
+    def __init__(self, names, refs):
+        for (name, _), ref in zip(names, refs, strict=True):
+            setattr(self, name, ref)
+
+
+def hbm(shape, dtype=jnp.bfloat16):
+    return jax.ShapeDtypeStruct(shape, dtype)
+
+
+GROUP = 4
+BACK_IN = [
+    (name, ANY)
+    for name in (
+        "hidden_t", "slope", "cot", "second_t", "second_unit", "att_t", "q", "k", "v", "o", "logsum", "first_t",
+        "first_unit", "joined_t", "w_skip", "w_joint", "w_up", "w_down", "cond_t",
+    )
+] + [
+    (name, pl.BlockSpec(memory_space=pltpu.VMEM))
+    for name in (
+        "second_rstd", "first_rstd", "gain_second", "gain_first", "seg_q", "seg_k", "cond_unit", "cond_rstd"
+    )
+]
+BACK_OUT = [
+    ("d_latents", hbm((TOK, WIDTH))),
+    ("d_skip", hbm((TOK, WIDTH))),
+    ("g_skip", hbm((2 * PART, WIDTH))),
+    ("g_joint", hbm((PART, 4 * WIDTH))),
+    ("g_up", hbm((PART, 4 * WIDTH))),
+    ("g_down", hbm((4 * PART, WIDTH))),
+    ("hidden_t2", hbm((4, 4, PART, TOK))),
+    ("second_t2", hbm((4, PART, TOK))),
+    ("att_t2", hbm((4, PART, TOK))),
+    ("first_t2", hbm((4, PART, TOK))),
+    ("joined_t2", hbm((4, 2 * PART, TOK))),
+]
+BACK_SCRATCH = [
+    ("cot_v", pltpu.VMEM((TOK, WIDTH), jnp.bfloat16)),
+    ("cot2", pltpu.VMEM((TOK, WIDTH), jnp.bfloat16)),
+    ("wide", pltpu.VMEM((4, TOK, WIDTH), jnp.bfloat16)),
+    ("before2", pltpu.VMEM((4, TOK, WIDTH), jnp.bfloat16)),
+    ("triple2", pltpu.VMEM((3, TOK, WIDTH), jnp.bfloat16)),
+    ("branch", pltpu.VMEM((TOK, WIDTH), jnp.bfloat16)),
+    ("branch2", pltpu.VMEM((TOK, WIDTH), jnp.bfloat16)),
+    ("base_g", pltpu.VMEM((TOK, WIDTH), jnp.bfloat16)),
+    ("base2", pltpu.VMEM((TOK, WIDTH), jnp.bfloat16)),
+    ("acc", pltpu.VMEM((TOK, WIDTH), jnp.float32)),
+    ("d_middle", pltpu.VMEM((TOK, WIDTH), jnp.float32)),
+    ("tile", pltpu.VMEM((TOK, WIDTH), jnp.bfloat16)),
+    ("weight", pltpu.VMEM((2, 8, PART, WIDTH), jnp.bfloat16)),
+    ("left", pltpu.VMEM((2, 4, PART, TOK), jnp.bfloat16)),
+    ("made", pltpu.VMEM((2, 4, PART, WIDTH), jnp.bfloat16)),
+    ("heads_g", pltpu.VMEM((HEADS, TOK, HEAD), jnp.bfloat16)),
+    ("qh", pltpu.VMEM((GROUP, TOK, HEAD), jnp.bfloat16)),
+    ("oh", pltpu.VMEM((GROUP, TOK, HEAD), jnp.bfloat16)),
+    ("kh", pltpu.VMEM((GROUP, HALO + TOK + COND, HEAD), jnp.bfloat16)),
+    ("vh", pltpu.VMEM((GROUP, HALO + TOK + COND, HEAD), jnp.bfloat16)),
+    ("lh", pltpu.VMEM((GROUP, TOK, 1), jnp.float32)),
+    ("sum_k", pltpu.VMEM((HALO + TOK + COND, HEAD), jnp.float32)),
+    ("sum_v", pltpu.VMEM((HALO + TOK + COND, HEAD), jnp.float32)),
+    ("bias", pltpu.VMEM((TOK, HALO + TOK + COND), jnp.float32)),
+    ("halo2", pltpu.VMEM((2, HALO, WIDTH), jnp.bfloat16)),
+    ("d_cond", pltpu.VMEM((128, 2 * WIDTH), jnp.bfloat16)),
+    ("cond_left", pltpu.VMEM((4, PART, 128), jnp.bfloat16)),
+    ("sums", pltpu.VMEM((16, WIDTH), jnp.float32)),
+    ("wide_sum", pltpu.VMEM((1, WIDTH), jnp.float32)),
+    ("w_sems", pltpu.SemaphoreType.DMA((2,))),
+    ("l_sems", pltpu.SemaphoreType.DMA((2,))),
+    ("m_sems", pltpu.SemaphoreType.DMA((2,))),
+    ("t_sems", pltpu.SemaphoreType.DMA((8,))),
+    ("sib_sems", pltpu.SemaphoreType.DMA((32, 2))),
+]
+SUM_SKIP, SUM_GAIN1, SUM_SHIFT1, SUM_OUT, SUM_GAIN2, SUM_SHIFT2, SUM_DOWN, SUM_UP = range(8)
+
+
+def back_greet(place):
+    barrier = pltpu.get_barrier_semaphore()
+    p = place
+    near = [p.at(x=1 - p.x), p.at(y=1 - p.y), p.at(c=1 - p.c)] + [p.at(zz=p.other(k)) for k in (1, 2, 3)]
+    for device in near:
+        pl.semaphore_signal(barrier, inc=1, device_id=device, device_id_type=MESH)
+    up = (p.c == 1) & (p.zz < 3)
+    down = (p.c == 0) & (p.zz > 0)
+    for go, device in ((up, (p.s, p.b + 1)), (down, (p.s, p.b - 1))):
+
+        @pl.when(go)
+        def _():
+            pl.semaphore_signal(barrier, inc=1, device_id=device, device_id_type=MESH)
+
+    pl.when(up | down)(lambda: pl.semaphore_wait(barrier, len(near) + 1))
+    pl.when(jnp.logical_not(up | down))(lambda: pl.semaphore_wait(barrier, len(near)))
+
+
+def back_kernel(*refs):
+    cuts = [len(BACK_IN), len(BACK_OUT), 2, len(Sum.PARTS), len(Sum.LANDS), len(BACK_SCRATCH), len(Sum.SEMS), 2]
+    pieces, at = [], 0
+    for cut in cuts:
+        pieces.append(refs[at : at + cut])
+        at += cut
+    i, o, b = Names(BACK_IN, pieces[0]), Names(BACK_OUT, pieces[1]), Names(BACK_SCRATCH, pieces[5])
+    p = Place()
+    total = Sum(p, pieces[3], pieces[4], (o.g_skip, o.g_joint, o.g_up, o.g_down), pieces[6], pieces[7])
+    vectors = Vectors(p, *pieces[2], refs[at:])
+    f32, bf16 = jnp.float32, jnp.bfloat16
+
+    def copy(src, dst, sem):
+        return pltpu.make_async_copy(src, dst, sem)
+
+    def sib(n, src, dst):
+        return remote(src, dst, b.sib_sems.at[n, 0], b.sib_sems.at[n, 1], p.at(c=1 - p.c))
+
+    def halves(n, src, dst):
+        return [sib(4 * n + zz, src.at[2 * zz + 1 - p.c], dst.at[zz]) for zz in range(4)]
+
+    left_pairs = (
+        (i.hidden_t, o.hidden_t2), (i.second_t, o.second_t2), (i.att_t, o.att_t2), (i.first_t, o.first_t2),
+        (i.joined_t, o.joined_t2),
+    )
+
+    def stream(blocks, body):
+        def load(n):
+            return copy(blocks[n], b.weight.at[n % 2], b.w_sems.at[n % 2])
+
+        load(0).start()
+        for n in range(len(blocks)):
+            if n + 1 < len(blocks):
+                load(n + 1).start()
+            load(n).wait()
+            body(n, b.weight[n % 2].reshape(WIDTH, WIDTH))
+
+    def column(ref, q):
+        return ref.at[:, :, pl.ds(q * WIDTH, WIDTH)]
+
+    def by_rows(size, body):
+        @pl.loop(0, TOK // size)
+        def _(n):
+            body(pl.ds(pl.multiple_of(n * size, size), size))
+
+    def add_sum(row, value):
+        b.sums[row : row + 1, :] += value
+
+    def colsum(value):
+        return jnp.sum(value, axis=0, keepdims=True)
+
+    def form(n, dst, own, own2, pairs, extra=None):
+        result = nn(own.reshape(4 * PART, TOK), pairs[0]) + nn(own2.reshape(4 * PART, TOK), pairs[1])
+        if extra is not None:
+            result += extra
+        slot = n % 2
+        b.made[slot] = result.astype(bf16).reshape(4, PART, WIDTH)
+        copy(b.made.at[slot], dst, b.m_sems.at[slot]).start()
+
+    def formed(n, dst):
+        copy(b.made.at[n % 2], dst, b.m_sems.at[n % 2]).wait()
+
+    def load_left(own, other):
+        one, two = copy(own, b.left.at[0], b.l_sems.at[0]), copy(other, b.left.at[1], b.l_sems.at[1])
+        one.start()
+        two.start()
+        one.wait()
+        two.wait()
+
+    def send_all(copies):
+        for one in copies:
+            one.start()
+
+    def recv_all(copies):
+        for one in copies:
+            one.wait_recv()
+
+    cot_load = copy(i.cot, b.cot_v, b.t_sems.at[0])
+    cot_load.start()
+    back_greet(p)
+    sib_cot = sib(20, i.cot, b.cot2)
+    left_sends = [halves(n, src, dst) for n, (src, dst) in enumerate(left_pairs)]
+    send_all(left_sends[0])
+    sib_cot.start()
+    for n in (1, 2, 3, 4):
+        send_all(left_sends[n])
+    b.sums[...] = jnp.zeros_like(b.sums)
+    b.d_cond[2 * COND :] = jnp.zeros((128 - 2 * COND, 2 * WIDTH), bf16)
+    vectors.part[...] = jnp.zeros_like(vectors.part)
+    make_bias(i.seg_q, i.seg_k, b.bias)
+    cot_load.wait()
+
+    def before_sib(q):
+        return sib(21 + q, b.wide.at[q], b.before2.at[q])
+
+    def slope_load(q):
+        return copy(i.slope.at[:, pl.ds(q * WIDTH, WIDTH)], b.tile, b.t_sems.at[1])
+
+    def do_before(q, weight):
+        slope_load(q).start()
+        b.acc[...] = nt(b.cot_v[...], weight)
+        slope_load(q).wait()
+        b.wide_sum[...] = jnp.zeros_like(b.wide_sum)
+
+        @functools.partial(by_rows, 64)
+        def _(rows):
+            value = (b.acc[rows] * b.tile[rows].astype(f32)).astype(bf16)
+            b.wide[q, rows] = value
+            b.wide_sum[...] += colsum(value.astype(f32))
+
+        for n in range(8):
+            row = 7 + n % 4
+            vectors.part[2 * q + n // 4, row : row + 1, 0:PART] = b.wide_sum[:, n * PART : (n + 1) * PART]
+        before_sib(q).start()
+
+    stream([i.w_down.at[pl.ds(8 * q, 8)] for q in range(4)], do_before)
+
+    sib_cot.wait_recv()
+    down_parts = pieces[3][3]
+    for n, zz in enumerate(ORDER):
+        left_sends[0][zz].wait_recv()
+        load_left(i.hidden_t.at[2 * zz + p.c], o.hidden_t2.at[zz])
+        form(n, down_parts.at[zz], b.left[0], b.left[1], (b.cot_v[...], b.cot2[...]))
+        if n > 0:
+            formed(n - 1, down_parts.at[ORDER[n - 1]])
+            total.start(3, (ORDER[n - 1],))
+    formed(3, down_parts.at[ORDER[3]])
+    total.start(3, (ORDER[3],))
+
+    def load_lefts(n):
+        own = [copy(left_pairs[n][0].at[2 * zz + p.c], b.left.at[0, zz], b.t_sems.at[4 + zz]) for zz in range(4)]
+        send_all(own)
+        recv_all_halves = left_sends[n]
+        for one in recv_all_halves:
+            one.wait_recv()
+        two = copy(left_pairs[n][1], b.left.at[1], b.l_sems.at[1])
+        two.start()
+        for one in own:
+            one.wait()
+        two.wait()
+
+    up_parts = pieces[3][2]
+    load_lefts(1)
+    for q in range(4):
+        before_sib(q).wait_recv()
+        form(q, column(up_parts, q), b.left[0], b.left[1], (b.wide[q], b.before2[q]))
+        if q > 0:
+            formed(q - 1, column(up_parts, q - 1))
+    formed(3, column(up_parts, 3))
+
+    def do_second(q, weight):
+        value = nt(b.wide[q], weight)
+        if q == 0:
+            b.acc[...] = value
+        else:
+            b.acc[...] += value
+
+    unit_load = copy(i.second_unit, b.tile, b.t_sems.at[1])
+    unit_load.start()
+    stream([column(i.w_up, q) for q in range(4)], do_second)
+    unit_load.wait()
+
+    def norm_rows(unit, rstd, gain, grad, gain_row, shift_row):
+        scaled = grad * gain
+        mean1 = jnp.mean(scaled, axis=1, keepdims=True)
+        mean2 = jnp.mean(scaled * unit, axis=1, keepdims=True)
+        add_sum(gain_row, colsum(grad * unit))
+        add_sum(shift_row, colsum(grad))
+        return rstd * (scaled - mean1 - unit * mean2)
+
+    @functools.partial(by_rows, 64)
+    def _(rows):
+        unit = b.tile[rows].astype(f32)
+        back = norm_rows(unit, i.second_rstd[rows], i.gain_second[...], b.acc[rows], SUM_GAIN2, SUM_SHIFT2)
+        g = b.cot_v[rows].astype(f32)
+        middle = g + back
+        b.d_middle[rows] = middle
+        low = middle.astype(bf16)
+        b.branch[rows] = low
+        add_sum(SUM_OUT, colsum(low.astype(f32)))
+        add_sum(SUM_DOWN, colsum(g))
+
+    branch_sib = sib(25, b.branch, b.branch2)
+    branch_sib.start()
+
+    def do_attended(_, weight):
+        b.tile[...] = nt(b.branch[...], weight).astype(bf16)
+        for h in range(HEADS):
+            b.heads_g[h] = b.tile[:, head(h)]
+
+    stream([column(i.w_joint, 3)], do_attended)
+
+    joint_parts = pieces[3][1]
+    load_lefts(2)
+    branch_sib.wait_recv()
+    form(0, column(joint_parts, 3), b.left[0], b.left[1], (b.branch[...], b.branch2[...]))
+    formed(0, column(joint_parts, 3))
+
+    total.pass_on(3)
+    total.start(2)
+    for q in range(4):
+        before_sib(q).wait_send()
+
+    scale = HEAD**-0.5
+    n_keys = HALO + TOK + COND
+
+    def group_loads(start):
+        hs = pl.ds(start, GROUP)
+        pairs = ((i.q, b.qh), (i.o, b.oh), (i.k, b.kh), (i.v, b.vh), (i.logsum, b.lh))
+        return [copy(src.at[hs], dst, b.t_sems.at[n]) for n, (src, dst) in enumerate(pairs)]
+
+    def group(start):
+        send_all(group_loads(start))
+        for one in group_loads(start):
+            one.wait()
+
+        @pl.loop(0, GROUP)
+        def _(h):
+            for row, low in TILES:
+                rows, keys = pl.ds(row, 256), pl.ds(low, n_keys - low)
+                q, k, v, g = b.qh[h, rows], b.kh[h, keys], b.vh[h, keys], b.heads_g[start + h, rows]
+                scores = nt(q, k) * (scale * LOG2E) + b.bias[rows, keys]
+                probs = jnp.exp2(scores - b.lh[h, rows])
+                d_probs = nt(g, v)
+                inner = jnp.sum(g.astype(f32) * b.oh[h, rows].astype(f32), axis=1, keepdims=True)
+                d_scores = (probs * (d_probs - inner)).astype(bf16)
+                d_k, d_v = tn(d_scores, q), tn(probs.astype(bf16), g)
+                if row == 0:
+                    b.sum_k[...] = d_k
+                    b.sum_v[...] = d_v
+                else:
+                    b.sum_k[keys] += d_k
+                    b.sum_v[keys] += d_v
+                b.oh[h, rows] = (nn(d_scores, k) * scale).astype(bf16)
+            b.kh[h] = (b.sum_k[...] * scale).astype(bf16)
+            b.vh[h] = b.sum_v[...].astype(bf16)
+
+        for n in range(GROUP):
+            at = head(start + n)
+            b.wide[0, :, at] = b.oh[n]
+            for j, made in ((0, b.kh), (1, b.vh)):
+                wide = slice(j * WIDTH + at.start, j * WIDTH + at.stop)
+                b.before2[j, 0:HALO, at] = made[n, 0:HALO]
+                b.wide[1 + j, :, at] = made[n, HALO : HALO + TOK]
+                b.d_cond[0:COND, wide] = made[n, HALO + TOK :]
+
+    group(0)
+    group(4)
+    total.to_chip(3)
+    group(8)
+    group(12)
+
+    def halo_copy(device):
+        src = b.before2.at[pl.ds(0, 2), pl.ds(0, HALO)]
+        return remote(src, b.halo2, b.sib_sems.at[31, 0], b.sib_sems.at[31, 1], device)
+
+    cond_sib = sib(30, b.d_cond.at[pl.ds(0, COND)], b.d_cond.at[pl.ds(COND, COND)])
+    cond_sib.start()
+    pl.when(p.b > 0)(lambda: halo_copy((p.s, p.b - 1)).start())
+
+    def triple_sib(j):
+        return sib(26 + j, b.wide.at[j], b.triple2.at[j])
+
+    triple_sib(0).start()
+    load_lefts(3)
+    for zz in range(4):
+        copy(i.cond_t.at[2 * zz + p.c], b.cond_left.at[zz], b.t_sems.at[zz]).start()
+
+    @pl.when(p.b < 7)
+    def _():
+        halo_copy((p.s, p.b)).wait_recv()
+
+        @pl.loop(0, HALO // 64)
+        def _(n):
+            low = pl.ds(pl.multiple_of(n * 64, 64), 64)
+            rows = pl.ds(pl.multiple_of(n * 64 + TOK - HALO, 64), 64)
+            for j in (0, 1):
+                extra = b.halo2[j, low].astype(f32)
+                b.wide[1 + j, rows] = (b.wide[1 + j, rows].astype(f32) + extra).astype(bf16)
+
+    triple_sib(1).start()
+    triple_sib(2).start()
+    for zz in range(4):
+        copy(i.cond_t.at[2 * zz + p.c], b.cond_left.at[zz], b.t_sems.at[zz]).wait()
+    cond_sib.wait_recv()
+
+    for j in range(3):
+        triple_sib(j).wait_recv()
+        extra = None
+        if j > 0:
+            extra = nn(b.cond_left[...].reshape(4 * PART, 128), b.d_cond[:, (j - 1) * WIDTH : j * WIDTH])
+        form(j, column(joint_parts, j), b.left[0], b.left[1], (b.wide[j], b.triple2[j]), extra)
+        if j > 0:
+            formed(j - 1, column(joint_parts, j - 1))
+    formed(2, column(joint_parts, 2))
+    total.pass_on(2, after=3)
+    total.start(1)
+    total.finish(3)
+
+    def do_first(j, weight):
+        value = nt(b.wide[j], weight)
+        if j == 0:
+            b.acc[...] = value
+        else:
+            b.acc[...] += value
+            cond = nt(b.d_cond[0:COND, (j - 1) * WIDTH : j * WIDTH], weight)
+            if j == 1:
+                vectors.mine[...] = cond
+            else:
+                vectors.mine[...] += cond
+
+    unit_load = copy(i.first_unit, b.tile, b.t_sems.at[1])
+    unit_load.start()
+    stream([column(i.w_joint, j) for j in range(3)], do_first)
+    unit_load.wait()
+
+    @functools.partial(by_rows, 64)
+    def _(rows):
+        unit = b.tile[rows].astype(f32)
+        back = norm_rows(unit, i.first_rstd[rows], i.gain_first[...], b.acc[rows], SUM_GAIN1, SUM_SHIFT1)
+        low = (b.d_middle[rows] + back).astype(bf16)
+        b.base_g[rows] = low
+        add_sum(SUM_SKIP, colsum(low.astype(f32)))
+
+    base_sib = sib(29, b.base_g, b.base2)
+    base_sib.start()
+    vectors.mine[...] = norm_rows(
+        i.cond_unit[...], i.cond_rstd[...], i.gain_first[...], vectors.mine[...], SUM_GAIN1, SUM_SHIFT1
+    )
+    for row in range(7):
+        for n in range(8):
+            vectors.part[n, row : row + 1, 0:PART] = b.sums[row : row + 1, n * PART : (n + 1) * PART]
+    vectors.run_pair()
+    total.to_chip(2, after=3)
+
+    skip_parts = pieces[3][0]
+    base_sib.wait_recv()
+    for n in (0, 1):
+        own = [
+            copy(
+                i.joined_t.at[2 * (2 * n + k // 2) + p.c, pl.ds((k % 2) * PART, PART)],
+                b.left.at[0, k],
+                b.t_sems.at[4 + k],
+            )
+            for k in range(4)
+        ]
+        for k in (0, 1):
+            left_sends[4][2 * n + k].wait_recv()
+        two = [
+            copy(
+                o.joined_t2.at[2 * n + k // 2, pl.ds((k % 2) * PART, PART)], b.left.at[1, k], b.t_sems.at[k]
+            )
+            for k in range(4)
+        ]
+        send_all(own + two)
+        for one in own + two:
+            one.wait()
+        form(n, skip_parts.at[pl.ds(4 * n, 4)], b.left[0], b.left[1], (b.base_g[...], b.base2[...]))
+    for n in (0, 1):
+        formed(n, skip_parts.at[pl.ds(4 * n, 4)])
+    vectors.run_x()
+
+    def do_joined(n, weight):
+        made = (b.tile, b.branch)[n]
+        made[...] = nt(b.base_g[...], weight).astype(bf16)
+        copy(made, (o.d_latents, o.d_skip)[n], b.t_sems.at[n]).start()
+
+    branch_sib.wait_send()
+    stream([i.w_skip.at[pl.ds(8 * n, 8)] for n in range(2)], do_joined)
+    vectors.run_y()
+
+    total.pass_on(1, after=2)
+    total.start(0)
+    total.finish(2)
+    total.to_chip(1, after=2)
+    total.pass_on(0, after=1)
+    total.finish(1)
+    total.to_chip(0, after=1)
+    total.finish(0)
+    vectors.run_z()
+    for n in (0, 1):
+        copy((b.tile, b.branch)[n], (o.d_latents, o.d_skip)[n], b.t_sems.at[n]).wait()
+    for group_sends in left_sends:
+        for one in group_sends:
+            one.wait_send()
+    for one in (sib_cot, cond_sib, base_sib, triple_sib(0), triple_sib(1), triple_sib(2)):
+        one.wait_send()
+    pl.when(p.b > 0)(lambda: halo_copy((p.s, p.b - 1)).wait_send())
+    for t in (3, 2, 1, 0):
+        total.done(t, t == 0)
+
+
+def backward(arrays):
+    vm = pl.BlockSpec(memory_space=pltpu.VMEM)
+    outs = pl.pallas_call(
+        back_kernel,
+        out_shape=[shape for _, shape in BACK_OUT] + [
+            jax.ShapeDtypeStruct(LITTLE, jnp.float32), jax.ShapeDtypeStruct((COND, WIDTH), jnp.bfloat16)
+        ] + Sum.PARTS + Sum.LANDS,
+        in_specs=[spec for _, spec in BACK_IN],
+        out_specs=[ANY] * len(BACK_OUT) + [vm] * 2 + [ANY] * (len(Sum.PARTS) + len(Sum.LANDS)),
+        scratch_shapes=[shape for _, shape in BACK_SCRATCH] + Sum.SEMS + Sum.SLOTS + Vectors.SCRATCH,
+        compiler_params=pltpu.CompilerParams(collective_id=1, has_side_effects=True, vmem_limit_bytes=60 << 20),
+    )(*[arrays[name] for name, _ in BACK_IN])
+    named = {name: out for (name, _), out in zip(BACK_OUT, outs)}
+    return named, outs[len(BACK_OUT)], outs[len(BACK_OUT) + 1]
+
+
+def item_ends(extra_length):
+    lengths = extra_length[0] + (LEN_MIN - 1)
+    count = lengths.shape[0]
+    upto = lax.iota(jnp.int32, count)[None, :] <= lax.iota(jnp.int32, count)[:, None]
+    return jnp.sum(jnp.where(upto, lengths[None, :], 0), axis=1)
+
+
+def norm_parts(values):
+    center = values - jnp.mean(values, axis=-1, keepdims=True)
+    spread = jnp.mean(center * center, axis=-1, keepdims=True)
+    rstd = lax.rsqrt(spread + 1e-05)
+    return center * rstd, rstd
+
+
+def quick(
+    latents, skip_input, cond_tokens, extra_length, skip_weight, skip_bias, first_gain, first_shift, joint_weight,
+    out_weight, out_bias, second_gain, second_shift, up_weight, up_bias, down_weight, down_bias, cotangent,
+):
+    f32, bf16 = jnp.float32, jnp.bfloat16
+    vectors = (skip_bias, first_gain, first_shift, out_bias, second_gain, second_shift, down_bias, up_bias)
+    packed = jnp.concatenate(vectors + (jnp.zeros((SMALL[0] * SMALL[1] - 11 * PART,), bf16),)).reshape(SMALL)
+    small, skip_all, joint_all, up_all, down_all = gather_weights(
+        packed, skip_weight, joint_weight, out_weight, up_weight, down_weight
+    )
+    small = small.reshape(8, SMALL[0] * SMALL[1])
+    skip_offset, gain_first, shift_first, out_offset, gain_second, shift_second, down_offset = (
+        v.reshape(WIDTH).astype(f32) for v in jnp.split(small[:, : 7 * PART], 7, axis=1)
+    )
+    up_offset = small[:, 7 * PART : 11 * PART].reshape(4 * WIDTH).astype(f32)
+    skip_matrix = skip_all.reshape(2 * WIDTH, WIDTH)
+    joint_out = joint_all.reshape(WIDTH, 4 * WIDTH)
+    joint_matrix, out_matrix = joint_out[:, : 3 * WIDTH], joint_out[:, 3 * WIDTH :]
+    up_matrix = up_all.reshape(WIDTH, 4 * WIDTH)
+    down_matrix = down_all.reshape(4 * WIDTH, WIDTH)
+
+    rows, width = latents.shape
+    here = lax.axis_index("blk")
+    ends = item_ends(extra_length)
+    places = here * rows + lax.iota(jnp.int32, HALO + rows) - HALO
+    items = jnp.where(places >= 0, jnp.sum((ends[None, :] <= places[:, None]).astype(jnp.int32), axis=1), -1)
+    seg_q = items[HALO:, None]
+    seg_k = jnp.concatenate([items, lax.iota(jnp.int32, COND) // 2])[None, :]
+
+    base = nn(latents, skip_matrix[:width]) + nn(skip_input, skip_matrix[width:]) + skip_offset
+    first_unit, first_rstd = norm_parts(base)
+    first_in = (first_unit * gain_first + shift_first).astype(bf16)
+    triple = nn(first_in, joint_matrix).astype(bf16)
+    cond_flat = cond_tokens.reshape(-1, width).astype(f32)
+    cond_unit, cond_rstd = norm_parts(cond_flat)
+    cond_in = (cond_unit * gain_first + shift_first).astype(bf16)
+    cond_pair = nn(cond_in, joint_matrix[:, width:]).astype(bf16)
+    halo = lax.ppermute(triple[rows - HALO :, width:], "blk", [(i, i + 1) for i in range(7)])
+    query, pairs = triple[:, :width], jnp.concatenate([halo, triple[:, width:], cond_pair], 0)
+    attended, logsum, heads_q, heads_k, heads_v, heads_o = attend(query, pairs, seg_q, seg_k)
+    middle = base + nn(attended, out_matrix) + out_offset
+    second_unit, second_rstd = norm_parts(middle)
+    second_in = (second_unit * gain_second + shift_second).astype(bf16)
+    before = nn(second_in, up_matrix) + up_offset
+    inside = 0.5 * (1.0 + lax.erf(before * 2**-0.5))
+    slope = (inside + before * jnp.exp(-0.5 * before * before) * (2 * jnp.pi) ** -0.5).astype(bf16)
+    hidden = (before * inside).astype(bf16)
+    hidden, slope = lax.optimization_barrier((hidden, slope))
+    output = middle + nn(hidden, down_matrix) + down_offset
+
+    cond_t = jnp.pad(jnp.concatenate([cond_in, cond_in], 0).T, ((0, 0), (0, 128 - 2 * COND)))
+    arrays = dict(
+        hidden_t=hidden.T.reshape(8, 4, PART, rows),
+        slope=slope,
+        cot=cotangent,
+        second_t=second_in.T.reshape(8, PART, rows),
+        second_unit=second_unit.astype(bf16),
+        att_t=attended.T.reshape(8, PART, rows),
+        q=heads_q,
+        k=heads_k,
+        v=heads_v,
+        o=heads_o,
+        logsum=logsum,
+        first_t=first_in.T.reshape(8, PART, rows),
+        first_unit=first_unit.astype(bf16),
+        joined_t=jnp.concatenate([latents.T, skip_input.T], 0).reshape(8, 2 * PART, rows),
+        w_skip=skip_all.reshape(16, PART, width),
+        w_joint=joint_all,
+        w_up=up_all,
+        w_down=down_all.reshape(32, PART, width),
+        cond_t=cond_t.reshape(8, PART, 128),
+        second_rstd=second_rstd,
+        first_rstd=first_rstd,
+        gain_second=gain_second[None],
+        gain_first=gain_first[None],
+        seg_q=seg_q,
+        seg_k=seg_k,
+        cond_unit=cond_unit,
+        cond_rstd=cond_rstd,
+    )
+    made, vector_sums, cond_sum = backward(arrays)
+    v = [vector_sums[n, :PART] for n in range(7)]
+    return (
+        output.astype(bf16),
+        made["d_latents"],
+        made["d_skip"],
+        cond_sum.reshape(cond_tokens.shape),
+        made["g_skip"].astype(f32),
+        v[0],
+        v[1],
+        v[2],
+        made["g_joint"][:, : 3 * WIDTH].astype(f32),
+        made["g_joint"][:, 3 * WIDTH :].astype(f32),
+        v[3],
+        v[4],
+        v[5],
+        made["g_up"].astype(f32),
+        vector_sums[7:11, :PART].reshape(-1),
+        made["g_down"].astype(f32),
+        v[6],
+    )
 
 
 def shifted(value, axis, steps):
@@ -52,7 +1325,7 @@
     return jnp.where(allowed, scores, -1e30)
 
 
-def shards(
+def plain(
     latents,
     skip_input,
     cond_tokens,
@@ -120,7 +1393,7 @@
         cond_in, joint_matrix[:, width:], preferred_element_type=jnp.float32
     ).astype(jnp.bfloat16)
     pairs = jnp.concatenate([pair_left, pair_here, cond_pair], 0)
-    ends = jnp.cumsum(extra_length[0] + (LEN_MIN - 1))
+    ends = item_ends(extra_length)
     here = lax.axis_index("blk")
     places = here * rows + lax.iota(jnp.int32, rows)
     seg_here = segment_ids(ends, places)
@@ -354,8 +1627,9 @@
         P("blk"),
         P(("stream", "blk"), None),
     )
+    fits = mesh.shape["stream"] == 4 and mesh.shape["blk"] == 8
     return jax.shard_map(
-        shards,
+        quick if fits else plain,
         mesh=mesh,
         in_specs=placed,
         out_specs=(

time: 1230 us -> 576 us (0.47)
  waiting for transfers between devices: 632 us -> 0.01 us
  Pallas kernels: 0 us -> 452 us
  matrix products: 355 us -> 42.9 us
  blocking collectives: 61.8 us -> 0 us
  other arithmetic: 60.8 us -> 23.1 us
  local copies, waits for them, and re-layouts: 80.4 us -> 46.2 us
  between operations: 18.1 us -> 1.39 us
    pallas_call x0 -> x3, Pallas kernels: none -> 452 us  [the longest x1 292 us: backward(): pl.pallas_call(back_kernel, out_shape=[shape for _, shape in BACK_OUT] +...]
    reduce_scatter x5 -> x0, waiting for transfers between devices: 350 us -> none  [the longest x1 111 us: shards(): lax.psum_scatter(grad_down_matrix.astype(jnp.bfloat16), 'blk', scatter_di...]
    dot_general x130 -> x7, matrix products: 355 us -> 42.9 us  [nn(): return jnp.dot(a, b, preferred_element_type=jnp.float32)]
    all_gather x5 -> x0, waiting for transfers between devices: 157 us -> none  [the longest x1 71.5 us: shards(): lax.all_gather(joint_weight, 'blk', axis=0, tiled=True)]
    ppermute x2 -> x1, waiting for transfers between devices: 69.7 us -> 0.01 us  [quick(): lax.ppermute(triple[rows - HALO:, width:], 'blk', [(i, i + 1) for i in ra...]
    psum x2 -> x0, waiting for transfers between devices: 52.6 us -> none  [the longest x1 52.6 us: shards(): lax.psum(share_skip.astype(jnp.bfloat16), 'stream').astype(jnp.float32)]
    unnamed x2 -> x0, blocking collectives: 52.2 us -> none
    dynamic_update_slice x16 -> x0, local copies, waits for them, and re-layouts: 21.5 us -> none  [shards(): mixed, logsum = lax.map(head_forward, (head_query, head_key, head_value))]
  transfers between devices with their start and end apart: 14 -> 1, of which waited for: 10 -> 0; matrix products, arithmetic and copies ran while one was open for 22% -> 4% of each run, Pallas kernels for 0% -> 0%
where the time goes in v2:
time: 576 us; the launch traced here: 568 us
  Pallas kernels  452 us (78%)
  local copies, waits for them, and re-layouts  46.2 us (8%)
  matrix products  42.9 us (7%)
  other arithmetic  23.1 us (4%)
    pallas_call x1, Pallas kernels, backward(): pl.pallas_call(back_kernel, out_shape=[shape for _, shape in BACK_OUT] +...  292 us
    pallas_call x1, Pallas kernels, gather_weights(): pl.pallas_call(gather_kernel, out_shape=[jax.ShapeDtypeStruct((8, *SMALL)...  131 us
    dot_general x7, matrix products, nn(): return jnp.dot(a, b, preferred_element_type=jnp.float32)  42.9 us
    pallas_call x1, Pallas kernels, attend(): pl.pallas_call(attend_kernel, out_shape=[jax.ShapeDtypeStruct((rows, HEAD...  29.4 us
  transfers between devices with their start and end apart: 1, of which 0 were waited for; matrix products, arithmetic and copies ran while one was open for 4% of the time, Pallas kernels for 0%

profile of v2, /device:TPU:12, one launch (start us, length us, event | category | flops | bytes accessed | tf_op | source)
XLA Modules:
  0.0 567.9 jit_solution(3013473556248644898)
XLA Ops:
  0.7 6.0 %concatenate.15 = bf16[2048]{0:T(1024)(128)(2,1)} concatenate(bf16[144]{0:T(256)(128)(2,1)} %param.23, bf16[144]{0:T(256)(128)(2,1)} %param.24, bf16[144]{0:T(256)(128)(2,1)} %param.25, bf16[144]{0:T(256)(128)(2,1)} %param.28, bf16[144]{0:T(256)(128)(2,1)} %param.29, bf16[144]{0:T(256)(128)(2,1)} %param.30, bf16[144]{0:T(256)(128)(2,1)} %param.34, bf16[576]{0:T(1024)(128)(2,1)} %param.32, ...), dimensions={0} | concatenate | bytes 8192 | tf_op jit(solution)/shard_map/concatenate | solution.py:1189
  6.7 131.0 %shard_map.305 = (bf16[8,16,128]{2,1,0:T(8,128)(2,1)}, bf16[8,288,1152]{2,1,0:T(8,128)(2,1)}, bf16[8,144,4608]{2,1,0:T(8,128)(2,1)}, bf16[8,144,4608]{2,1,0:T(8,128)(2,1)}, bf16[8,576,1152]{2,1,0:T(8,128)(2,1)}) custom-call(bf16[16,128]{1,0:T(8,128)(2,1)} %bitcast.102, bf16[288,1152]{1,0:T(8,128)(2,1)} %refs_1_.1, bf16[144,3456]{1,0:T(8,128)(2,1)} %refs_2_.2, ...), custom_call_target="tpu_custom_call" | custom-call | tf_op jit(solution)/shard_map/pallas_call | solution.py:289
  138.8 3.1 fusion.40
  142.0 1.8 fusion.43
  143.8 2.0 fusion.42
  146.3 5.5 fusion.7
  152.0 1.6 copy-done.6
  153.6 2.3 collective-permute-start
  156.5 2.8 pad_maximum_fusion.1
  162.3 1.4 slice.98.query
  164.0 4.6 copy.64
  173.5 3.5 fusion.12
  177.0 3.2 pad_maximum_fusion.pairs
  180.2 29.4 %shard_map.306 = (bf16[512,1152]{1,0:T(8,128)(2,1)S(1)}, f32[16,512,1]{2,1,0:T(8,128)}, bf16[16,512,72]{2,1,0:T(8,128)(2,1)}, bf16[16,864,72]{2,1,0:T(8,128)(2,1...) custom-call(bf16[512,1152]{1,0:T(8,128)(2,1)S(1)} %slice.98.query, ...), custom_call_target="tpu_custom_call" | custom-call | tf_op jit(solution)/shard_map/pallas_call | solution.py:364
  209.6 1.4 copy.62
  211.0 5.5 fusion.38
  217.0 1.3 multiply_convert_fusion.1.refs_4_
  218.3 1.1 copy-done.3
  219.5 2.0 add_convert_fusion
  221.5 2.5 copy.63
  224.0 1.5 copy.66.refs_19_
  225.5 1.4 copy.61
  227.0 14.2 %fusion.4 = (bf16[512,4608]{1,0:T(8,128)(2,1)}, bf16[512,4608]{1,0:T(8,128)(2,1)}) fusion(f32[4608]{0:T(1024)} %reshape.290, bf16[1152,4608]{1,0:T(8,128)(2,1)} %bitcast.84, f32[512,1152]{1,0:T(8,128)S(1)} %copy-done.5, f32[1152]{0:T(1024)} %reshape.289, f32[1152]{0:T(1024)S(1)} %copy-done.20, f32[512]{0:T(512)S(1)} %copy-done.18, f32[512]{0:T(512)S(1)} %copy-done.16), kind=kOutput, calls=%fused_computation.5 | convolution fusion | flops 5467078656 | bytes 22445056 | tf_op jit(solution)/shard_map/dot_general | solution.py:323
  241.1 6.7 %copy.60 = bf16[4608,512]{1,0:T(8,128)(2,1)} copy(bf16[4608,512]{0,1:T(8,128)(2,1)} %bitcast.86) | data formatting | bytes 9437184 | tf_op jit(solution)/shard_map/transpose | solution.py:1235
  247.8 291.7 %shard_map.307 = (bf16[512,1152]{1,0:T(8,128)(2,1)}, bf16[512,1152]{1,0:T(8,128)(2,1)}, bf16[288,1152]{1,0:T(8,128)(2,1)}, bf16[144,4608]{1,0:T(8,128)(2,1)}, bf...) custom-call(bf16[8,4,144,512]{3,2,1,0:T(8,128)(2,1)} %bitcast.76, ...), custom_call_target="tpu_custom_call" | custom-call | tf_op jit(solution)/shard_map/pallas_call | solution.py:1155
  540.3 1.5 fusion.41
  541.9 1.9 slice_convert_fusion.1
  543.7 2.6 slice_convert_fusion
  547.7 1.1 convert_element_type.200
  548.8 4.1 convert_element_type.203
  552.9 1.7 convert_element_type.204
  554.6 10.3 %fusion.17 = bf16[512,1152]{1,0:T(8,128)(2,1)} fusion(f32[512,1152]{1,0:T(8,128)S(1)} %copy-done.5, bf16[512,4608]{1,0:T(8,128)(2,1)S(1)} %bitcast.88, bf16[4608,1152]{1,0:T(8,128)(2,1)} %bitcast.78, f32[1152]{0:T(1024)S(1)} %copy-done.28), kind=kOutput, calls=%fused_computation.19 | convolution fusion | flops 5437587456 | bytes 18878976 | tf_op jit(solution)/shard_map/dot_general | solution.py:323
  (122 shorter events, 15.7 us)
Async XLA Ops:
  138.8 3.1 copy-start.10
  138.8 5.0 copy-start.11
  141.9 4.3 slice-start
  141.9 4.3 slice-start.1
  143.8 2.4 slice-start.2
  145.8 6.0 %copy-start.2 = (f32[1152,512]{0,1:T(8,128)}, f32[1152,512]{0,1:T(8,128)S(1)}, u32[]{:S(2)}) copy-start(f32[1152,512]{0,1:T(8,128)S(1)} %get-tuple-element.85) | copy-start | bytes 7077892
  145.8 65.2 %copy-start.24 = (f32[512]{0:T(512)}, f32[512]{0:T(512)S(1)}, u32[]{:S(2)}) copy-start(f32[512]{0:T(512)S(1)} %broadcast_multiply_fusion.2) | copy-start | bytes 6148
  146.2 64.8 %copy-start.26 = (f32[512]{0:T(512)}, f32[512]{0:T(512)S(1)}, u32[]{:S(2)}) copy-start(f32[512]{0:T(512)S(1)} %add_rsqrt_fusion.2) | copy-start | bytes 6148
  151.8 4.0 copy-start.29
  151.8 4.3 copy-start.12
  153.6 23.4 %collective-permute-start = (bf16[320,2304]{1,0:T(8,128)(2,1)S(1)}, bf16[320,2304]{1,0:T(8,128)(2,1)}, u32[]{:S(2)}, u32[]{:S(2)}) collective-permute-start(bf16[320,2304]{1,0:T(8,128)(2,1)S(1)} %slice.99), channel_id=1, source_target_pairs={{0,1},{1,2},{2,3},{3,4},{4,5},{5,6},{6,7},{8,9},{9,10},{10,11},{11... | collective-permute-start | bytes 4423688 | tf_op jit(solution)/shard_map/ppermute | solution.py:1220
  163.8 16.4 %copy-start.1 = (s32[1,864]{1,0:T(1,128)}, s32[1,864]{1,0:T(1,128)S(1)}, u32[]{:S(2)}) copy-start(s32[1,864]{1,0:T(1,128)S(1)} %broadcast_in_dim.30.seg_k.refs_24_) | copy-start | bytes 10372
  164.0 16.2 %copy-start = (s32[512,1]{1,0:T(8,128)}, s32[512,1]{1,0:T(8,128)S(1)}, u32[]{:S(2)}) copy-start(s32[512,1]{1,0:T(8,128)S(1)} %copy.59.seg_q.refs_23_) | copy-start | bytes 6148
  170.8 40.2 %copy-start.22 = (f32[1152]{0:T(1024)}, f32[1152]{0:T(1024)S(1)}, u32[]{:S(2)}) copy-start(f32[1152]{0:T(1024)S(1)} %reshape.287) | copy-start | bytes 13828
  173.5 3.5 slice-start.3
  216.9 2.5 copy-start.3
  216.9 2.5 copy-start.19
  216.9 2.5 copy-start.21
  216.9 2.5 copy-start.23
  217.0 2.5 copy-start.25
  217.0 2.5 copy-start.27
  217.0 4.5 copy-start.17
  221.5 5.5 copy-start.5
  221.5 5.5 copy-start.16
  221.5 5.5 copy-start.18
  221.5 5.5 copy-start.20
  539.5 7.5 %copy-start.14 = (bf16[32,1152]{1,0:T(8,128)(2,1)S(1)}, bf16[32,1152]{1,0:T(8,128)(2,1)}, u32[]{:S(2)}) copy-start(bf16[32,1152]{1,0:T(8,128)(2,1)} %get-tuple-element.53) | copy-start | bytes 221188
  539.5 8.2 %copy-start.13 = (bf16[288,1152]{1,0:T(8,128)(2,1)S(1)}, bf16[288,1152]{1,0:T(8,128)(2,1)}, u32[]{:S(2)}) copy-start(bf16[288,1152]{1,0:T(8,128)(2,1)} %get-tuple-element.54) | copy-start | bytes 1990660
  547.7 6.9 %slice-start.4 = ((s8[4718592]{0:T(1024)(128)(4,1)}), s8[4194304]{0:T(1024)(128)(4,1)S(1)}, s32[]{:S(2)}) async-start(s8[4718592]{0:T(1024)(128)(4,1)} %bitcast.87), calls=%async_computation.4 | async-start | bytes 8388608
  548.8 4.1 copy-start.7
  548.8 5.8 %slice-start.5 = ((s8[4718592]{0:T(1024)(128)(4,1)}), s8[524288]{0:T(1024)(128)(4,1)S(1)}, s32[]{:S(2)}) async-start(s8[4718592]{0:T(1024)(128)(4,1)} %bitcast.87), calls=%async_computation.5 | async-start | bytes 1048576
  554.6 10.4 %copy-start.9 = (bf16[512,1152]{1,0:T(8,128)(2,1)S(1)}, bf16[512,1152]{1,0:T(8,128)(2,1)}, u32[]{:S(2)}) copy-start(bf16[512,1152]{1,0:T(8,128)(2,1)} %get-tuple-element.105) | copy-start | bytes 3538948
  (5 other events, 8.7 us)
